TPU v7x, 128 devices: a whole 4x4x4 slice. The times are simulated.
128 devices in a mesh: cells: 16 (over y_lo, x, core), spots: 8 (over y_hi, z).
Axes of the slice: x: 4, y: 4 (y_hi: 2, y_lo: 2; y = y_hi * 2 + y_lo), z: 4, core: 2. Of those that a mesh axis runs over, the one named last changes fastest.
Arguments:
- cell_feat: bfloat16 [16384, 64], P('cells')
- spot_feat: bfloat16 [32768, 64], P('spots')
- cell_mass: float32 [16384], P('cells'), may hold values from 0.02 to 5
- spot_mass: float32 [32768], P('spots'), may hold values from 0.02 to 5
- block_pattern: int32 [128, 256], P('cells', 'spots'), may hold values from 0 to 1, as said below
Outputs:
- cell_pot: float32 [16384], P('cells')
- spot_pot: float32 [32768], P('spots')
- cell_map: float32 [16384, 64], P('cells')
- spot_map: float32 [32768, 64], P('spots')
Inputs may be any that keep to these rules, and one draw needn't show every extreme that they name: `block_pattern`: every cluster block row and every cluster block column holds at least one allowed pair; the share of allowed blocks differs between cell cluster rows.
All inputs are finite; a program needn't handle non-finite values.
Results may differ from a plain program's by a relative error of at most 0.0024.
Values sent between devices are 32-bit elements; how exact they have to be, the bound alone decides.
A program may use at most 64 MiB of HBM per device.

v0:
```python
import jax
import jax.numpy as jnp
from jax import lax
from jax.sharding import PartitionSpec as P

FEAT = 64
CLUSTER = 128
ITERS = 5


EPSILON = 0.05
NEG = -1e30


def merged(value, axis, combine):
    everything = jax.tree.map(lambda part: lax.all_gather(part, axis), value)
    leading = jax.tree.map(lambda part: part[0], everything)

    def step(k, so_far):
        return combine(so_far, jax.tree.map(lambda part: part[k], everything))

    return lax.fori_loop(1, lax.axis_size(axis), step, leading)


def allowed_tile(pattern):
    count_a, count_b = pattern.shape
    full = jnp.broadcast_to(pattern[:, None, :, None] > 0, (count_a, CLUSTER, count_b, CLUSTER))
    return full.reshape(count_a * CLUSTER, count_b * CLUSTER)


def partial_side(own_feat, own_norm, other_feat, other_norm, other_pot, pattern, mapped):
    count_own = own_feat.shape[0]
    count_other = other_feat.shape[0]
    width = own_feat.shape[1]
    row_span = min(512, count_own)
    col_span = min(1024, count_other)
    row_blocks = count_own // row_span
    col_blocks = count_other // col_span
    feat_blocks = own_feat.reshape(row_blocks, row_span, width)
    norm_blocks = own_norm.reshape(row_blocks, row_span)
    pattern_blocks = pattern.reshape(row_blocks, row_span // CLUSTER, pattern.shape[1])

    def one_block(items):
        feat_b, norm_b, pattern_b = items

        def advance(index, carry):
            start = index * col_span
            feat_c = lax.dynamic_slice_in_dim(other_feat, start, col_span, 0)
            norm_c = lax.dynamic_slice_in_dim(other_norm, start, col_span, 0)
            pot_c = lax.dynamic_slice_in_dim(other_pot, start, col_span, 0)
            pattern_c = lax.dynamic_slice_in_dim(
                pattern_b, index * (col_span // CLUSTER), col_span // CLUSTER, 1
            )
            cross = lax.dot_general(
                feat_b, feat_c, (((1,), (1,)), ((), ())), preferred_element_type=jnp.float32
            )
            cost = (norm_b[:, None] + norm_c[None, :] - 2.0 * cross) / FEAT
            score = (pot_c[None, :] - cost) / EPSILON
            allow = allowed_tile(pattern_c)
            peak = carry[0]
            new_peak = jnp.maximum(peak, jnp.max(jnp.where(allow, score, NEG), axis=1))
            weights = jnp.where(allow, jnp.exp(score - new_peak[:, None]), 0.0)
            factor = jnp.exp(peak - new_peak)
            total = carry[1] * factor + jnp.sum(weights, axis=1)
            if mapped:
                product = jnp.dot(
                    weights.astype(jnp.bfloat16), feat_c, preferred_element_type=jnp.float32
                )
                return (new_peak, total, carry[2] * factor[:, None] + product)
            return (new_peak, total)

        start_peak = jnp.full((row_span,), NEG, jnp.float32)
        start_total = jnp.zeros((row_span,), jnp.float32)
        if mapped:
            init = (start_peak, start_total, jnp.zeros((row_span, width), jnp.float32))
        else:
            init = (start_peak, start_total)
        return lax.fori_loop(0, col_blocks, advance, init)

    result = lax.map(one_block, (feat_blocks, norm_blocks, pattern_blocks))
    peak = result[0].reshape(count_own)
    total = result[1].reshape(count_own)
    if mapped:
        return (peak, total, result[2].reshape(count_own, width))
    return (peak, total, None)


def join_plain(first, second):
    top = jnp.maximum(first[0], second[0])
    return (top, first[1] * jnp.exp(first[0] - top) + second[1] * jnp.exp(second[0] - top))


def join_mapped(first, second):
    top = jnp.maximum(first[0], second[0])
    scale_a = jnp.exp(first[0] - top)
    scale_b = jnp.exp(second[0] - top)
    return (
        top,
        first[1] * scale_a + second[1] * scale_b,
        first[2] * scale_a[:, None] + second[2] * scale_b[:, None],
    )


def finish(mass, peak, total):
    return EPSILON * (jnp.log(mass) - peak - jnp.log(total))


def row_reduce(peak, total, weighted, mass, mapped):
    if mapped:
        peak, total, weighted = merged((peak, total, weighted), "spots", join_mapped)
        return (finish(mass, peak, total), weighted / total[:, None])
    peak, total = merged((peak, total), "spots", join_plain)
    return (finish(mass, peak, total), None)


def col_reduce(peak, total, weighted, mass, mapped):
    if mapped:
        peak, total, weighted = merged((peak, total, weighted), "cells", join_mapped)
        return (finish(mass, peak, total), weighted / total[:, None])
    peak, total = merged((peak, total), "cells", join_plain)
    return (finish(mass, peak, total), None)


def per_device(cell_feat, spot_feat, cell_mass, spot_mass, block_pattern):
    cell_norm = jnp.sum(cell_feat.astype(jnp.float32) ** 2, axis=1)
    spot_norm = jnp.sum(spot_feat.astype(jnp.float32) ** 2, axis=1)
    pattern_cols = block_pattern.T
    spot_pot = jnp.zeros((spot_feat.shape[0],), jnp.float32)
    cell_map = None
    spot_map = None
    for step in range(ITERS):
        mapped = step == ITERS - 1
        peak, total, weighted = partial_side(
            cell_feat, cell_norm, spot_feat, spot_norm, spot_pot, block_pattern, mapped
        )
        cell_pot, cell_map = row_reduce(peak, total, weighted, cell_mass, mapped)
        peak, total, weighted = partial_side(
            spot_feat, spot_norm, cell_feat, cell_norm, cell_pot, pattern_cols, mapped
        )
        spot_pot, spot_map = col_reduce(peak, total, weighted, spot_mass, mapped)
    return (cell_pot, spot_pot, cell_map, spot_map)


def solution(mesh):
    in_specs = (P("cells", None), P("spots", None), P("cells"), P("spots"), P("cells", "spots"))
    out_specs = (P("cells"), P("spots"), P("cells", None), P("spots", None))
    return jax.shard_map(
        per_device, mesh=mesh, in_specs=in_specs, out_specs=out_specs, check_vma=False
    )
```

profile of v0, /device:TPU:1, one launch (start us, length us, event | category | flops | bytes accessed | tf_op | source)
XLA Modules:
  0.0 982.3 jit_solution(15799421828088179869)
XLA Ops:
  10.5 25.6 %while.412 = (s32[]{:T(128)}, f32[2,512]{1,0:T(2,128)S(1)}, f32[2,512]{1,0:T(2,128)S(1)}, s32[2,4,32]{2,1,0:T(4,128)}, bf16[2,512,64]{2,1,0:T(8,128)(2,1)S(1)}, ...) while((s32[]{:T(128)}, f32[2,512]{1,0:T(2,128)S(1)}, ...), condition=%wide.region_7.8_spmd, body=%wide.region_2.7_spmd.sunk | while | flops 72878632 | bytes 6150377 | solution.py:80
  36.1 30.1 %all-gather = f32[8,1,1024]{2,1,0:T(1,128)S(1)} all-gather(f32[1,1,1024]{2,1,0:T(1,128)S(1)} %reshape.381), channel_id=1, replica_groups=mesh['cells'=16,'spots'=8] {'spots'}, dimensions={0}, use_global_device_ids=true | all-gather | bytes 36864 | tf_op jit(solution)/shard_map/all_gather | solution.py:16
  66.2 27.7 %all-gather.1 = f32[8,1,1024]{2,1,0:T(1,128)S(1)} all-gather(f32[1,1,1024]{2,1,0:T(1,128)S(1)} %reshape.383), channel_id=1, replica_groups=mesh['cells'=16,'spots'=8] {'spots'}, dimensions={0}, use_global_device_ids=true | all-gather | bytes 36864 | tf_op jit(solution)/shard_map/all_gather | solution.py:16
  113.2 32.9 %all-gather.2 = f32[16,1,4096]{2,1,0:T(1,128)S(1)} all-gather(f32[1,1,4096]{2,1,0:T(1,128)S(1)} %reshape.385), channel_id=1, replica_groups=mesh['cells'=16,'spots'=8] {'cells'}, dimensions={0}, use_global_device_ids=true | all-gather | bytes 278528 | tf_op jit(solution)/shard_map/all_gather | solution.py:16
  182.2 28.2 %all-gather.4 = f32[8,1,1024]{2,1,0:T(1,128)S(1)} all-gather(f32[1,1,1024]{2,1,0:T(1,128)S(1)} %reshape.389), channel_id=1, replica_groups=mesh['cells'=16,'spots'=8] {'spots'}, dimensions={0}, use_global_device_ids=true | all-gather | bytes 36864 | tf_op jit(solution)/shard_map/all_gather | solution.py:16
  210.4 27.7 %all-gather.5 = f32[8,1,1024]{2,1,0:T(1,128)S(1)} all-gather(f32[1,1,1024]{2,1,0:T(1,128)S(1)} %reshape.391), channel_id=1, replica_groups=mesh['cells'=16,'spots'=8] {'spots'}, dimensions={0}, use_global_device_ids=true | all-gather | bytes 36864 | tf_op jit(solution)/shard_map/all_gather | solution.py:16
  255.1 30.8 %all-gather.6 = f32[16,1,4096]{2,1,0:T(1,128)S(1)} all-gather(f32[1,1,4096]{2,1,0:T(1,128)S(1)} %reshape.393), channel_id=1, replica_groups=mesh['cells'=16,'spots'=8] {'cells'}, dimensions={0}, use_global_device_ids=true | all-gather | bytes 278528 | tf_op jit(solution)/shard_map/all_gather | solution.py:16
  304.6 17.4 %while.422 = (s32[]{:T(128)}, f32[2,512]{1,0:T(2,128)S(1)}, f32[2,512]{1,0:T(2,128)S(1)}, s32[2,4,32]{2,1,0:T(4,128)S(1)}, bf16[2,512,64]{2,1,0:T(8,128)(2,1)S(1...) while((s32[]{:T(128)}, f32[2,512]{1,0:T(2,128)S(1)}, ...), condition=%wide.region_35.36_spmd, body=%wide.region_30.35_spmd.sunk | while | flops 72878632 | bytes 6228229 | solution.py:80
  322.0 28.0 %all-gather.8 = f32[8,1,1024]{2,1,0:T(1,128)S(1)} all-gather(f32[1,1,1024]{2,1,0:T(1,128)S(1)} %reshape.397), channel_id=1, replica_groups=mesh['cells'=16,'spots'=8] {'spots'}, dimensions={0}, use_global_device_ids=true | all-gather | bytes 36864 | tf_op jit(solution)/shard_map/all_gather | solution.py:16
  350.1 27.7 %all-gather.9 = f32[8,1,1024]{2,1,0:T(1,128)S(1)} all-gather(f32[1,1,1024]{2,1,0:T(1,128)S(1)} %reshape.399), channel_id=1, replica_groups=mesh['cells'=16,'spots'=8] {'spots'}, dimensions={0}, use_global_device_ids=true | all-gather | bytes 36864 | tf_op jit(solution)/shard_map/all_gather | solution.py:16
  394.7 30.8 %all-gather.10 = f32[16,1,4096]{2,1,0:T(1,128)S(1)} all-gather(f32[1,1,4096]{2,1,0:T(1,128)S(1)} %reshape.401), channel_id=1, replica_groups=mesh['cells'=16,'spots'=8] {'cells'}, dimensions={0}, use_global_device_ids=true | all-gather | bytes 278528 | tf_op jit(solution)/shard_map/all_gather | solution.py:16
  444.1 17.4 %while.427 = (s32[]{:T(128)}, f32[2,512]{1,0:T(2,128)S(1)}, f32[2,512]{1,0:T(2,128)S(1)}, s32[2,4,32]{2,1,0:T(4,128)S(1)}, bf16[2,512,64]{2,1,0:T(8,128)(2,1)S(1...) while((s32[]{:T(128)}, f32[2,512]{1,0:T(2,128)S(1)}, ...), condition=%wide.region_49.50_spmd, body=%wide.region_44.49_spmd.sunk | while | flops 72878632 | bytes 6228229 | solution.py:80
  461.5 28.0 %all-gather.12 = f32[8,1,1024]{2,1,0:T(1,128)S(1)} all-gather(f32[1,1,1024]{2,1,0:T(1,128)S(1)} %reshape.405), channel_id=1, replica_groups=mesh['cells'=16,'spots'=8] {'spots'}, dimensions={0}, use_global_device_ids=true | all-gather | bytes 36864 | tf_op jit(solution)/shard_map/all_gather | solution.py:16
  489.5 27.7 %all-gather.13 = f32[8,1,1024]{2,1,0:T(1,128)S(1)} all-gather(f32[1,1,1024]{2,1,0:T(1,128)S(1)} %reshape.407), channel_id=1, replica_groups=mesh['cells'=16,'spots'=8] {'spots'}, dimensions={0}, use_global_device_ids=true | all-gather | bytes 36864 | tf_op jit(solution)/shard_map/all_gather | solution.py:16
  534.8 30.7 %all-gather.14 = f32[16,1,4096]{2,1,0:T(1,128)S(1)} all-gather(f32[1,1,4096]{2,1,0:T(1,128)S(1)} %reshape.409), channel_id=1, replica_groups=mesh['cells'=16,'spots'=8] {'cells'}, dimensions={0}, use_global_device_ids=true | all-gather | bytes 278528 | tf_op jit(solution)/shard_map/all_gather | solution.py:16
  584.4 24.9 %while.432 = (s32[]{:T(128)}, f32[2,512]{1,0:T(2,128)S(1)}, f32[2,512]{1,0:T(2,128)S(1)}, f32[2,512,64]{1,0,2:T(2,128)S(1)}, s32[2,4,32]{2,1,0:T(4,128)S(1)}, /*...) while((s32[]{:T(128)}, f32[2,512]{1,0:T(2,128)S(1)}, ...), condition=%wide.region_63.64_spmd, body=%wide.region_58.63_spmd.sunk | while | flops 141658656 | bytes 9773350 | solution.py:80
  610.3 28.0 %all-gather.17 = f32[8,1,1024]{2,1,0:T(1,128)S(1)} all-gather(f32[1,1,1024]{2,1,0:T(1,128)S(1)} %reshape.415), channel_id=1, replica_groups=mesh['cells'=16,'spots'=8] {'spots'}, dimensions={0}, use_global_device_ids=true | all-gather | bytes 36864 | tf_op jit(solution)/shard_map/all_gather | solution.py:16
  639.5 27.7 %all-gather.16 = f32[8,1,1024]{2,1,0:T(1,128)S(1)} all-gather(f32[1,1,1024]{2,1,0:T(1,128)S(1)} %reshape.413), channel_id=1, replica_groups=mesh['cells'=16,'spots'=8] {'spots'}, dimensions={0}, use_global_device_ids=true | all-gather | bytes 36864 | tf_op jit(solution)/shard_map/all_gather | solution.py:16
  669.6 26.3 %while.433 = (s32[]{:T(128)}, f32[1024]{0:T(1024)}, f32[1024]{0:T(1024)}, f32[1024,64]{1,0:T(8,128)S(1)}, f32[8,1024]{1,0:T(8,128)}, /*index=5*/f32[8,1024]{1,0:...) while((s32[]{:T(128)}, f32[1024]{0:T(1024)}, f32[1024]{0:T(1024)}, ...), condition=%wide.region_65.66_spmd, body=%wide.region_64.65_spmd.sunk | while | flops 202757 | bytes 1892495 | solution.py:22
  696.6 48.8 %while.434 = (s32[]{:T(128)}, f32[8,512]{1,0:T(8,128)S(1)}, f32[8,512]{1,0:T(8,128)S(1)}, f32[8,512,64]{1,0,2:T(8,128)S(1)}, s32[8,4,8]{2,1,0:T(4,128)}, /*index...) while((s32[]{:T(128)}, f32[8,512]{1,0:T(8,128)S(1)}, ...), condition=%wide.region_69.70_spmd, body=%wide.region_66.69_spmd.sunk | while | flops 141592608 | bytes 9482581 | solution.py:80
  746.7 31.0 %all-gather.19 = f32[16,1,4096]{2,1,0:T(1,128)S(1)} all-gather(f32[1,1,4096]{2,1,0:T(1,128)S(1)} %reshape.419), channel_id=1, replica_groups=mesh['cells'=16,'spots'=8] {'cells'}, dimensions={0}, use_global_device_ids=true | all-gather | bytes 278528 | tf_op jit(solution)/shard_map/all_gather | solution.py:16
  778.6 17.5 %all-gather.18 = f32[16,1,4096]{2,1,0:T(1,128)S(1)} all-gather(f32[1,1,4096]{2,1,0:T(1,128)S(1)} %reshape.417), channel_id=1, replica_groups=mesh['cells'=16,'spots'=8] {'cells'}, dimensions={0}, use_global_device_ids=true | all-gather | bytes 278528 | tf_op jit(solution)/shard_map/all_gather | solution.py:16
  798.5 54.2 %all-gather.25.cloned.1.call-done = f32[16,4096,64]{1,2,0:T(8,128)} async-done(((f32[1,4096,64]{1,2,0:T(8,128)}), f32[16,4096,64]{1,2,0:T(8,128)}) %all-gather.25.cloned.1.call-update) | async-done | bytes 16777232 | tf_op jit(solution)/shard_map/all_gather | solution.py:16
  856.0 115.6 %while.435 = (s32[]{:T(128)}, f32[4096]{0:T(1024)S(1)}, f32[4096]{0:T(1024)S(1)}, f32[4096,64]{1,0:T(8,128)}, f32[16,4096]{1,0:T(8,128)}, /*index=5*/f32[16,4096...) while((s32[]{:T(128)}, f32[4096]{0:T(1024)S(1)}, f32[4096]{0:T(1024)S(1)}, ...), condition=%wide.region_71.72_spmd, body=%wide.region_70.71_spmd.sunk | while | flops 811013 | bytes 7569551 | solution.py:22
  (1349 shorter events, 636.8 us)
Async XLA Ops:
  7.2 661.3 %all-gather.23.cloned.1.call-start = ((), (), s32[]{:S(2)}) async-start(), calls=%async_computation | async-start | bytes 2359296 | tf_op jit(solution)/shard_map/all_gather | solution.py:16
  36.0 60.6 %copy-start.8 = (f32[1024]{0:T(1024)S(1)}, f32[1024]{0:T(1024)}, u32[]{:S(2)}) copy-start(f32[1024]{0:T(1024)} %param.57) | copy-start | bytes 12292
  36.0 60.6 %copy-start.2 = (bf16[1024,64]{0,1:T(8,128)(2,1)S(1)}, bf16[1024,64]{0,1:T(8,128)(2,1)}, u32[]{:S(2)}) copy-start(bf16[1024,64]{0,1:T(8,128)(2,1)} %param.55) | copy-start | bytes 393220
  113.2 51.5 %copy-start.3 = (f32[4096]{0:T(1024)S(1)}, f32[4096]{0:T(1024)}, u32[]{:S(2)}) copy-start(f32[4096]{0:T(1024)} %param.58) | copy-start | bytes 49156
  113.2 51.6 %copy-start = (bf16[4096,64]{0,1:T(8,128)(2,1)S(1)}, bf16[4096,64]{0,1:T(8,128)(2,1)}, u32[]{:S(2)}) copy-start(bf16[4096,64]{0,1:T(8,128)(2,1)} %get-tuple-element.5923) | copy-start | bytes 1572868
  113.2 51.6 %copy-start.1 = (s32[2,4,32]{2,1,0:T(4,128)S(1)}, s32[2,4,32]{2,1,0:T(4,128)}, u32[]{:S(2)}) copy-start(s32[2,4,32]{2,1,0:T(4,128)} %get-tuple-element.5959) | copy-start | bytes 3076
  534.2 0.6 copy-start.5
  534.2 0.6 copy-start.6
  534.2 50.2 %copy-start.9 = (f32[1024]{0:T(1024)}, f32[1024]{0:T(1024)S(1)}, u32[]{:S(2)}) copy-start(f32[1024]{0:T(1024)S(1)} %get-tuple-element.5980) | copy-start | bytes 12292
  534.2 50.2 %copy-start.7 = (f32[2,512,64]{1,0,2:T(2,128)S(1)}, f32[2,512,64]{1,0,2:T(2,128)}, u32[]{:S(2)}) copy-start(f32[2,512,64]{1,0,2:T(2,128)} %custom-call.11) | copy-start | bytes 786436
  610.2 242.5 %all-gather.25.cloned.1.call-start = ((), (), s32[]{:S(2)}) async-start(), calls=%async_computation.1 | async-start | bytes 17825792 | tf_op jit(solution)/shard_map/all_gather | solution.py:16
  745.4 1.2 copy-start.10
  971.6 3.3 copy-start.4
Sparse Core Ops, SparseCore 0:
  610.4 53.3 all-gather.22
  746.8 105.9 all-gather.24
where the time goes:
time: 987 us; the launch traced here: 982 us
  blocking collectives  523 us (53%)
  other arithmetic  149 us (15%)
  local copies, waits for them, and re-layouts  133 us (13%)
  matrix products  100 us (10%)
  waiting for transfers between devices  54.3 us (6%)
  between operations  14.7 us (1%)
    all_gather x20, blocking collectives, merged(): everything = jax.tree.map(lambda part: lax.all_gather(part, axis), value)  523 us
    dot_general x80, matrix products, advance(): lax.dot_general(feat_b, feat_c, (((1,), (1,)), ((), ())), preferred_eleme...  89.9 us
    add x22, other arithmetic, join_mapped(): first[2] * scale_a[:, None] + second[2] * scale_b[:, None]  74.7 us
    dynamic_slice x154, local copies, waits for them, and re-layouts, step(): return combine(so_far, jax.tree.map(lambda part: part[k], everything))  59.2 us
    all_gather x2, waiting for transfers between devices, merged(): everything = jax.tree.map(lambda part: lax.all_gather(part, axis), value)  54.2 us
    reduce_sum x80, other arithmetic, advance(): total = carry[1] * factor + jnp.sum(weights, axis=1)  49.4 us
    broadcast_in_dim x80, local copies, waits for them, and re-layouts, allowed_tile(): jnp.broadcast_to(pattern[:, None, :, None] > 0, (count_a, CLUSTER, count_...  21.8 us
  transfers between devices with their start and end apart: 2, of which 1 were waited for; matrix products, arithmetic and copies ran while one was open for 1% of the time, Pallas kernels for 0%

commit v1 on v0

v1 whole, which is shorter than its diff:
```python
import functools
import math

import jax
import jax.numpy as jnp
from jax import lax
from jax.experimental import pallas as pl
from jax.experimental.pallas import tpu as pltpu
from jax.sharding import PartitionSpec as P

FEAT = 64
BLK = 128
ITERS = 5
EPSILON = 0.05
NEG = -1e30
LOG2E = math.log2(math.e)
UNIT = LOG2E / EPSILON
CROSS = UNIT * 2.0 / FEAT
NORM = UNIT / FEAT
SIDE = 16
MSG = FEAT + 8
MESH = pl.DeviceIdType.MESH
F32 = jnp.float32
BF16 = jnp.bfloat16


def log2(v):
    return jnp.log(v) * LOG2E


def wait_for(view, sem):
    pltpu.make_async_copy(view, view, sem).wait()


def send(src, dst, ssem, rsem, dev):
    pltpu.make_async_remote_copy(
        src_ref=src, dst_ref=dst, send_sem=ssem, recv_sem=rsem, device_id=dev, device_id_type=MESH
    ).start()


def within(index, top):
    return jnp.minimum(jnp.maximum(index, 0), top)


def ring(offset):
    return {0: 0, 1: 1, 2: 2, 3: 1}[offset]


def lane_spread(pot, out):
    full = jnp.concatenate([pot, jnp.zeros((BLK - SIDE, BLK), F32)], axis=0)
    turned = jnp.transpose(full)
    for b in range(SIDE):
        out[b] = jnp.broadcast_to(turned[:, b : b + 1], (BLK, BLK))


def sinkhorn_kernel(
    cap, cfeat, sfeat, cmass, smass, pattern,
    cpot_out, spot_out, cmap_out, smap_out, flag_out,
    swap_out, swap_in, side_out, side_in, chh, cht, shh, sht, cross, crosst, spread,
    blockmap, slot_peak, peak_scr, list_v, list_s, tab_v, tab_s,
    buf_e, buf_d, flag_e, flag_d, msg_c, rcv_c, msg_s, rcv_s, own_c, own_s, pot_s,
    sem_swap, sem_e, sem_d, sem_map, sem_loc,
):
    ci = lax.axis_index("cells")
    si = lax.axis_index("spots")
    core = ci % 2
    dme = ci // 2
    ylo, xx = dme // 4, dme % 4
    yhi, zz = si // 4, si % 4
    eme = si * 2 + core
    partner = (ci + 1 - 2 * core, si)

    e_peers = []
    for a in range(2):
        for b in range(4):
            for k in range(2):
                if a or b or k:
                    s2 = lax.rem(yhi + a, 2) * 4 + lax.rem(zz + b, 4)
                    k2 = lax.rem(core + k, 2)
                    e_peers.append((2 * a + ring(b) + 0.1 * k, (dme * 2 + k2, s2), s2, k2))
    e_peers.sort(key=lambda item: -item[0])
    d_peers = []
    for a in range(2):
        for b in range(4):
            if a or b:
                d2 = lax.rem(ylo + a, 2) * 4 + lax.rem(xx + b, 4)
                d_peers.append((a + ring(b), (d2 * 2 + core, si), d2))
    d_peers.sort(key=lambda item: -item[0])

    barrier = pltpu.get_barrier_semaphore()
    for item in e_peers + d_peers:
        pl.semaphore_signal(barrier, inc=1, device_id=item[1], device_id_type=MESH)

    def own_cells(b, _):
        block = cfeat[:, pl.ds(pl.multiple_of(b * BLK, BLK), BLK)]
        wide = block.astype(F32)
        swap_out[b] = wide
        chh[core * 8 + b] = block
        cht[core * 8 + b] = jnp.transpose(wide).astype(BF16)
        return 0

    lax.fori_loop(0, 8, own_cells, 0)

    def own_spots(b, norms):
        block = sfeat[:, pl.ds(pl.multiple_of((core * SIDE + b) * BLK, BLK), BLK)]
        wide = block.astype(F32)
        shh[b] = block
        sht[b] = jnp.transpose(wide).astype(BF16)
        here = lax.broadcasted_iota(jnp.int32, (SIDE, BLK), 0) == b
        return jnp.where(here, jnp.sum(wide * wide, axis=0, keepdims=True) * NORM, norms)

    spot_norm = lax.fori_loop(0, SIDE, own_spots, jnp.zeros((SIDE, BLK), F32))
    pattern_own = (pattern[...] > 0).astype(F32)
    side_out[0] = cmass[...]
    side_out[1] = jnp.concatenate([pattern_own, jnp.zeros((8, BLK - 32), F32)], axis=1)

    pl.semaphore_wait(barrier, len(e_peers) + len(d_peers))

    send(side_out, side_in, sem_swap.at[0], sem_swap.at[1], partner)
    send(swap_out, swap_in, sem_swap.at[2], sem_swap.at[3], partner)
    wait_for(side_in, sem_swap.at[1])

    first = core == 0
    mine, theirs = side_out[1], side_in[1]
    lane = lax.broadcasted_iota(jnp.int32, (SIDE, BLK), 1)
    both = jnp.concatenate(
        [jnp.where(first, mine, theirs), jnp.where(first, theirs, mine)], axis=0
    )
    both = jnp.where((lane >= core * SIDE) & (lane < core * SIDE + SIDE), both, 0.0)
    upto = (
        lax.broadcasted_iota(jnp.int32, (BLK, BLK), 0)
        < lax.broadcasted_iota(jnp.int32, (BLK, BLK), 1)
    ).astype(BF16)
    inside = jnp.dot(both.astype(BF16), upto, preferred_element_type=F32)
    per_row = jnp.broadcast_to(jnp.sum(both, axis=1, keepdims=True), (SIDE, BLK))
    earlier = (
        lax.broadcasted_iota(jnp.int32, (SIDE, SIDE), 1)
        < lax.broadcasted_iota(jnp.int32, (SIDE, SIDE), 0)
    ).astype(BF16)
    before = jnp.dot(earlier, per_row.astype(BF16), preferred_element_type=F32)
    place = jnp.where(both > 0, before + inside, -1.0)
    count = jnp.sum(jnp.sum(both, axis=1, keepdims=True), axis=0, keepdims=True)
    over = jnp.broadcast_to(jnp.where(count > cap, 1.0, 0.0), (8, BLK))
    width = list_v.shape[1]
    pairs = SIDE * SIDE
    wide_place = jnp.broadcast_to(place[:, None, :], (SIDE, SIDE, BLK)).reshape(pairs, BLK)
    pair = lax.broadcasted_iota(jnp.int32, (pairs, BLK), 0)
    pair_lane = lax.broadcasted_iota(jnp.int32, (pairs, BLK), 1)
    chosen = pair_lane == core * SIDE + pair % SIDE
    slot_of = jnp.sum(jnp.where(chosen, wide_place, 0.0), axis=1, keepdims=True)
    hot = slot_of == lax.broadcasted_iota(jnp.int32, (pairs, width), 1).astype(F32)
    kind = lax.broadcasted_iota(jnp.int32, (8, pairs), 0)
    which = lax.broadcasted_iota(jnp.int32, (8, pairs), 1)
    facts = jnp.where(kind == 0, which // SIDE, jnp.where(kind == 1, which % SIDE, 1))
    lists = jnp.dot(
        facts.astype(F32).astype(BF16), hot.astype(F32).astype(BF16), preferred_element_type=F32
    )
    none = 99.0 * (1.0 - lists[2:3])
    kind = lax.broadcasted_iota(jnp.int32, (8, width), 0)
    lists = jnp.where(kind >= 2, 0.0, lists) + jnp.where(
        kind == 2, lists[0:1] + none, jnp.where(kind == 3, lists[1:2] + none, 0.0)
    )
    list_v[...] = lists.astype(jnp.int32)
    tab_v[...] = jnp.where((place < 0) | (place >= cap), float(cap), place).astype(jnp.int32)
    copies = [
        pltpu.make_async_copy(list_v, list_s, sem_loc.at[0]),
        pltpu.make_async_copy(tab_v, tab_s, sem_loc.at[1]),
    ]
    for copy in copies:
        copy.start()
    flag_e[eme] = over
    for _, dev, _, _ in e_peers:
        send(flag_e.at[eme], flag_e.at[eme], sem_e.at[0, ITERS], sem_e.at[1, ITERS], dev)

    cell_log = log2(
        jnp.concatenate(
            [
                jnp.where(first, side_out[0], side_in[0]),
                jnp.where(first, side_in[0], side_out[0]),
            ],
            axis=0,
        )
    )
    spot_log = log2(smass[pl.ds(pl.multiple_of(core * SIDE, SIDE), SIDE), :])

    lane_spread(-spot_norm, spread)
    wait_for(swap_in, sem_swap.at[3])

    def other_cells(b, _):
        wide = swap_in[b]
        chh[(1 - core) * 8 + b] = wide.astype(BF16)
        cht[(1 - core) * 8 + b] = jnp.transpose(wide).astype(BF16)
        return 0

    lax.fori_loop(0, 8, other_cells, 0)
    for copy in copies:
        copy.wait()

    step = 4

    def build(i, _):
        for k in range(step):
            e = i * step + k
            r = within(list_s[0, e], SIDE - 1)
            c = within(list_s[1, e], SIDE - 1)
            cross[e] = jnp.dot(cht[r], shh[c], preferred_element_type=F32) * CROSS
            crosst[e] = jnp.dot(sht[c], chh[r], preferred_element_type=F32) * CROSS
        return 0

    lax.fori_loop(0, cap // step, build, 0)

    rows = lax.broadcasted_iota(jnp.int32, (SIDE, BLK), 0)

    def half(scores, other, own, feats):
        def body(i, carry):
            peak, total = carry
            parts = []
            for k in range(step):
                e = i * step + k
                o = within(list_s[other, e], SIDE - 1)
                v = scores[e] + spread[o]
                top = jnp.max(v, axis=0, keepdims=True)
                p = jnp.exp2(v - top)
                parts.append((list_s[own + 2, e], top, jnp.sum(p, axis=0, keepdims=True)))
                if feats is not None:
                    slot_peak[e] = top
                    blockmap[e] = jnp.dot(
                        feats[o], p.astype(BF16), preferred_element_type=F32
                    )
            for at, top, part in parts:
                new = jnp.where(rows == at, jnp.maximum(peak, top), peak)
                total = total * jnp.exp2(peak - new) + jnp.where(
                    rows == at, part * jnp.exp2(top - new), 0.0
                )
                peak = new
            return peak, total

        init = (jnp.full((SIDE, BLK), NEG, F32), jnp.zeros((SIDE, BLK), F32))
        return lax.fori_loop(0, cap // step, body, init)

    def joined(peak, total):
        return jnp.where(total > 0, peak + log2(jnp.maximum(total, 1e-30)), NEG)

    def merge(buf, it, n):
        top = buf[it, 0]
        for k in range(1, n):
            top = jnp.maximum(top, buf[it, k])
        total = jnp.exp2(buf[it, 0] - top)
        for k in range(1, n):
            total = total + jnp.exp2(buf[it, k] - top)
        return top + log2(total)

    def cell_start(it, feats):
        peak, total = half(crosst, 1, 0, feats)
        buf_e[it, eme] = joined(peak, total)
        for _, dev, _, _ in e_peers:
            send(buf_e.at[it, eme], buf_e.at[it, eme], sem_e.at[0, it], sem_e.at[1, it], dev)
        return peak, total

    def cell_end(it):
        wait_for(buf_e.at[it, pl.ds(0, 15)], sem_e.at[1, it])
        pot = cell_log - merge(buf_e, it, 16)
        lane_spread(pot, spread)
        return pot

    def iteration(it, _):
        cell_start(it, None)
        cell_end(it)
        peak, total = half(cross, 0, 1, None)
        buf_d[it, dme] = joined(peak, total)
        for _, dev, _ in d_peers:
            send(buf_d.at[it, dme], buf_d.at[it, dme], sem_d.at[0, it], sem_d.at[1, it], dev)
        wait_for(buf_d.at[it, pl.ds(0, 7)], sem_d.at[1, it])
        lane_spread(spot_log - merge(buf_d, it, 8), spread)
        return 0

    lax.fori_loop(0, ITERS - 1, iteration, 0)

    wait_for(flag_e.at[pl.ds(0, 15)], sem_e.at[1, ITERS])
    over = flag_e[0]
    for k in range(1, 16):
        over = jnp.maximum(over, flag_e[k])
    flag_d[dme] = over
    for _, dev, _ in d_peers:
        send(flag_d.at[dme], flag_d.at[dme], sem_d.at[0, ITERS], sem_d.at[1, ITERS], dev)

    def gather_maps(peak, total, msg, transposed):
        peak_scr[...] = peak
        blockmap[cap] = jnp.zeros((FEAT, BLK), F32)
        slot_peak[cap] = jnp.full((1, BLK), NEG, F32)

        def one(b, _):
            top = peak_scr[pl.ds(b, 1), :]
            acc = jnp.zeros((FEAT, BLK), F32)
            for k in range(SIDE):
                e = tab_s[k, core * SIDE + b] if transposed else tab_s[b, core * SIDE + k]
                e = within(e, cap)
                acc = acc + blockmap[e] * jnp.exp2(slot_peak[e] - top)
            msg[b, pl.ds(0, FEAT), :] = acc
            return 0

        lax.fori_loop(0, SIDE, one, 0)
        for b in range(SIDE):
            msg[b, pl.ds(FEAT, 8), :] = jnp.concatenate(
                [peak[b : b + 1], total[b : b + 1], jnp.zeros((6, BLK), F32)], axis=0
            )

    def total_map(take, n):
        top = take(0, pl.ds(FEAT, 8))[0:1]
        for k in range(1, n):
            top = jnp.maximum(top, take(k, pl.ds(FEAT, 8))[0:1])
        total = jnp.zeros((1, BLK), F32)
        acc = jnp.zeros((FEAT, BLK), F32)
        for k in range(n):
            stat = take(k, pl.ds(FEAT, 8))
            scale = jnp.exp2(stat[0:1] - top)
            total = total + stat[1:2] * scale
            acc = acc + take(k, pl.ds(0, FEAT)) * scale
        return top + log2(total), acc / total

    peak, total = cell_start(ITERS - 1, shh)
    gather_maps(peak, total, msg_c, False)
    for _, dev, s2, k2 in e_peers:
        send(msg_c.at[k2 * 8 + s2], rcv_c.at[eme], sem_map.at[0], sem_map.at[1], dev)
    rcv_c[eme] = msg_c[core * 8 + si]
    cell_pot = cell_end(ITERS - 1)

    peak, total = half(cross, 0, 1, chh)
    gather_maps(peak, total, msg_s, True)
    for _, dev, d2 in d_peers:
        send(msg_s.at[pl.ds(d2 * 2, 2)], rcv_s.at[dme], sem_map.at[2], sem_map.at[3], dev)
    rcv_s[dme] = msg_s[pl.ds(dme * 2, 2)]

    wait_for(rcv_c.at[pl.ds(0, 15)], sem_map.at[1])
    _, block = total_map(lambda k, r: rcv_c[k, r, :], 16)
    own_c[...] = block
    at = pl.ds(pl.multiple_of(si * BLK, BLK), BLK)
    cmap_out[:, at] = block
    for a in range(2):
        for b in (2, 1, 3, 0):
            if a or b:
                s2 = lax.rem(yhi + a, 2) * 4 + lax.rem(zz + b, 4)
                send(own_c, cmap_out.at[:, at], sem_map.at[4], sem_map.at[5], (ci, s2))

    wait_for(rcv_s.at[pl.ds(0, 7)], sem_map.at[3])
    lses = []
    for h in range(2):
        lse, block = total_map(lambda k, r: rcv_s[k, h, r, :], 8)
        own_s[:, pl.ds(h * BLK, BLK)] = block
        lses.append(lse)
    pot_s[dme] = jnp.concatenate(lses + [jnp.zeros((6, BLK), F32)], axis=0)
    half_at = core * SIDE * BLK
    at = pl.ds(pl.multiple_of(half_at + dme * 2 * BLK, 2 * BLK), 2 * BLK)
    smap_out[:, at] = own_s[...]
    for _, dev, _ in d_peers:
        send(pot_s.at[dme], pot_s.at[dme], sem_map.at[6], sem_map.at[7], dev)
        send(own_s, smap_out.at[:, at], sem_map.at[8], sem_map.at[9], dev)

    cell_norm = jnp.zeros((8, BLK), F32)
    rows8 = lax.broadcasted_iota(jnp.int32, (8, BLK), 0)
    for b in range(8):
        wide = swap_out[b]
        cell_norm = jnp.where(
            rows8 == b, jnp.sum(wide * wide, axis=0, keepdims=True) * NORM, cell_norm
        )
    cell_own = jnp.where(first, cell_pot[0:8], cell_pot[8:16])
    cpot_out[...] = (cell_own + cell_norm) * (1.0 / UNIT)

    wait_for(pot_s.at[pl.ds(0, 7)], sem_map.at[7])
    lse = jnp.concatenate([pot_s[k, 0:2, :] for k in range(8)], axis=0)
    half_rows = pl.ds(pl.multiple_of(core * SIDE, SIDE), SIDE)
    spot_out[half_rows, :] = (spot_log - lse + spot_norm) * (1.0 / UNIT)
    send(spot_out.at[half_rows], spot_out.at[half_rows], sem_swap.at[4], sem_swap.at[5], partner)
    half_cols = pl.ds(pl.multiple_of(half_at, SIDE * BLK), SIDE * BLK)
    part = smap_out.at[:, pl.ds(0, 7 * 2 * BLK)]
    wait_for(part, sem_map.at[9])
    send(smap_out.at[:, half_cols], smap_out.at[:, half_cols], sem_swap.at[6], sem_swap.at[7], partner)

    wait_for(flag_d.at[pl.ds(0, 7)], sem_d.at[1, ITERS])
    over = flag_d[0]
    for k in range(1, 8):
        over = jnp.maximum(over, flag_d[k])
    flag_out[...] = over

    wait_for(cmap_out.at[:, pl.ds(0, 7 * BLK)], sem_map.at[5])
    wait_for(spot_out.at[pl.ds(0, SIDE)], sem_swap.at[5])
    wait_for(smap_out.at[:, pl.ds(0, SIDE * BLK)], sem_swap.at[7])
    wait_for(side_out, sem_swap.at[0])
    wait_for(swap_out, sem_swap.at[2])
    wait_for(spot_out.at[pl.ds(0, SIDE)], sem_swap.at[4])
    wait_for(smap_out.at[:, pl.ds(0, SIDE * BLK)], sem_swap.at[6])
    wait_for(rcv_c.at[pl.ds(0, 15)], sem_map.at[0])
    wait_for(rcv_s.at[pl.ds(0, 7)], sem_map.at[2])
    wait_for(cmap_out.at[:, pl.ds(0, 7 * BLK)], sem_map.at[4])
    wait_for(pot_s.at[pl.ds(0, 7)], sem_map.at[6])
    wait_for(part, sem_map.at[8])
    wait_for(flag_e.at[pl.ds(0, 15)], sem_e.at[0, ITERS])
    wait_for(flag_d.at[pl.ds(0, 7)], sem_d.at[0, ITERS])

    def sent(it, _):
        wait_for(buf_e.at[it, pl.ds(0, 15)], sem_e.at[0, it])
        wait_for(buf_d.at[it, pl.ds(0, 7)], sem_d.at[0, it])
        return 0

    lax.fori_loop(0, ITERS - 1, sent, 0)
    wait_for(buf_e.at[ITERS - 1, pl.ds(0, 15)], sem_e.at[0, ITERS - 1])


def run(cap, collective, cfeat, sfeat, cmass, smass, pattern):
    width = 128 if cap <= 128 else 256
    vmem = lambda *shape: pltpu.VMEM(shape, F32)
    half = lambda *shape: pltpu.VMEM(shape, BF16)
    shape = lambda *dims: jax.ShapeDtypeStruct(dims, F32)
    scratch = [
        vmem(8, FEAT, BLK), vmem(8, FEAT, BLK), vmem(2, 8, BLK), vmem(2, 8, BLK),
        half(SIDE, FEAT, BLK), half(SIDE, BLK, FEAT), half(SIDE, FEAT, BLK), half(SIDE, BLK, FEAT),
        vmem(cap, BLK, BLK), vmem(cap, BLK, BLK), vmem(SIDE, BLK, BLK),
        vmem(cap + 1, FEAT, BLK), vmem(cap + 1, 1, BLK), vmem(SIDE, BLK),
        pltpu.VMEM((8, width), jnp.int32), pltpu.SMEM((8, width), jnp.int32),
        pltpu.VMEM((SIDE, BLK), jnp.int32), pltpu.SMEM((SIDE, BLK), jnp.int32),
        vmem(ITERS, 16, SIDE, BLK), vmem(ITERS - 1, 8, SIDE, BLK), vmem(16, 8, BLK), vmem(8, 8, BLK),
        vmem(SIDE, MSG, BLK), vmem(16, MSG, BLK), vmem(SIDE, MSG, BLK), vmem(8, 2, MSG, BLK),
        vmem(FEAT, BLK), vmem(FEAT, 2 * BLK), vmem(8, 8, BLK),
        pltpu.SemaphoreType.DMA((8,)), pltpu.SemaphoreType.DMA((2, ITERS + 1)),
        pltpu.SemaphoreType.DMA((2, ITERS + 1)), pltpu.SemaphoreType.DMA((10,)),
        pltpu.SemaphoreType.DMA((2,)),
    ]
    return pl.pallas_call(
        functools.partial(sinkhorn_kernel, cap),
        out_shape=(shape(8, BLK), shape(32, BLK), shape(FEAT, 1024), shape(FEAT, 4096), shape(8, BLK)),
        in_specs=[pl.BlockSpec(memory_space=pltpu.VMEM)] * 5,
        out_specs=tuple([pl.BlockSpec(memory_space=pltpu.VMEM)] * 5),
        scratch_shapes=scratch,
        compiler_params=pltpu.CompilerParams(
            collective_id=collective, has_side_effects=True, vmem_limit_bytes=60 * 2**20
        ),
    )(cfeat, sfeat, cmass, smass, pattern)


def per_device(cell_feat, spot_feat, cell_mass, spot_mass, block_pattern):
    args = (cell_feat.T, spot_feat.T, cell_mass.reshape(8, BLK), spot_mass.reshape(32, BLK), block_pattern)
    outs = run(56, 0, *args)
    cpot, spot, cmap, smap, _ = lax.while_loop(
        lambda now: now[4][0, 0] > 0, lambda now: run(SIDE * SIDE, 1, *args), outs
    )
    return cpot.reshape(1024), spot.reshape(4096), cmap.T, smap.T


def solution(mesh):
    in_specs = (P("cells", None), P("spots", None), P("cells"), P("spots"), P("cells", "spots"))
    out_specs = (P("cells"), P("spots"), P("cells", None), P("spots", None))
    return jax.shard_map(
        per_device, mesh=mesh, in_specs=in_specs, out_specs=out_specs, check_vma=False
    )
```

time: 987 us -> 109 us (0.11)
  blocking collectives: 523 us -> 0 us
  other arithmetic: 149 us -> 0 us
  local copies, waits for them, and re-layouts: 133 us -> 8.35 us
  matrix products: 100 us -> 0 us
  Pallas kernels: 0 us -> 98.5 us
  waiting for transfers between devices: 54.3 us -> 0 us
  between operations: 14.7 us -> 0.71 us
    all_gather x20 -> x0, blocking collectives: 523 us -> none  [merged(): everything = jax.tree.map(lambda part: lax.all_gather(part, axis), value)]
    dot_general x96 -> x0, matrix products: 100 us -> none  [the longest x80 89.9 us: advance(): lax.dot_general(feat_b, feat_c, (((1,), (1,)), ((), ())), preferred_eleme...]
    pallas_call x0 -> x1, Pallas kernels: none -> 98.5 us  [run(): pl.pallas_call(functools.partial(sinkhorn_kernel, cap), out_shape=(shape(...]
    add x212 -> x0, other arithmetic: 87 us -> none  [the longest x22 74.7 us: join_mapped(): first[2] * scale_a[:, None] + second[2] * scale_b[:, None]]
    dynamic_slice x356 -> x0, local copies, waits for them, and re-layouts: 71.9 us -> none  [the longest x154 59.2 us: step(): return combine(so_far, jax.tree.map(lambda part: part[k], everything))]
    all_gather x2 -> x0, waiting for transfers between devices: 54.2 us -> none  [merged(): everything = jax.tree.map(lambda part: lax.all_gather(part, axis), value)]
    reduce_sum x82 -> x0, other arithmetic: 51.6 us -> none  [the longest x80 49.4 us: advance(): total = carry[1] * factor + jnp.sum(weights, axis=1)]
    broadcast_in_dim x80 -> x0, local copies, waits for them, and re-layouts: 21.8 us -> none  [allowed_tile(): jnp.broadcast_to(pattern[:, None, :, None] > 0, (count_a, CLUSTER, count_...]
  transfers between devices with their start and end apart: 2 -> 0, of which waited for: 1 -> 0; matrix products, arithmetic and copies ran while one was open for 1% -> 0% of each run, Pallas kernels for 0% -> 0%
where the time goes in v1:
time: 109 us; the launch traced here: 108 us
  Pallas kernels  98.5 us (90%)
  local copies, waits for them, and re-layouts  8.35 us (8%)
    pallas_call x1, Pallas kernels, run(): pl.pallas_call(functools.partial(sinkhorn_kernel, cap), out_shape=(shape(...  98.5 us
    unnamed x16, local copies, waits for them, and re-layouts  7.16 us

profile of v1, /device:TPU:1, one launch (start us, length us, event | category | flops | bytes accessed | tf_op | source)
XLA Modules:
  0.0 108.2 jit_solution(18299704207858997066)
XLA Ops:
  0.6 0.0 copy-start.3
  0.6 0.0 copy-start
  0.7 0.7 copy-done.3
  1.3 0.0 copy-start.1
  1.3 0.0 copy-start.2
  1.3 98.5 %shard_map.84 = (f32[8,128]{1,0:T(8,128)}, f32[32,128]{1,0:T(8,128)}, f32[64,1024]{1,0:T(8,128)}, f32[64,4096]{1,0:T(8,128)}, f32[8,128]{1,0:T(8,128)}) custom-call(bf16[64,1024]{1,0:T(8,128)(2,1)} %bitcast.11, bf16[64,4096]{1,0:T(8,128)(2,1)} %bitcast.9, f32[8,128]{1,0:T(8,128)S(1)} %bitcast.17, f32[32,128]{1,0:T(8,128)} %bitcast.14, s32[8,32]{1,0:T(8,128)} %pattern.1), custom_call_target="tpu_custom_call" | custom-call | tf_op jit(solution)/shard_map/pallas_call | solution.py:428
  99.9 0.0 copy-start.4
  99.9 0.0 copy-done
  99.9 0.0 copy-done.1
  99.9 0.0 copy-done.2
  99.9 0.6 copy-done.4
  100.5 1.8 %while.15 = (f32[8,128]{1,0:T(8,128)}, f32[32,128]{1,0:T(8,128)}, f32[64,1024]{1,0:T(8,128)}, f32[64,4096]{1,0:T(8,128)}, f32[8,128]{1,0:T(8,128)}, /*index=5*/b...) while((f32[8,128]{1,0:T(8,128)}, f32[32,128]{1,0:T(8,128)}, ...), condition=%region_1.0_spmd, body=%region_0.0_spmd | while | flops 1 | bytes 97 | solution.py:443
  100.5 1.2 %slice.2 = f32[1,1]{1,0:T(1,128)} slice(f32[8,128]{1,0:T(8,128)} %get-tuple-element.50), slice={[0:1], [0:1]} | slice | bytes 8 | tf_op jit(solution)/shard_map/while/cond/slice | solution.py:444
  102.4 0.0 copy-start.5
  102.4 1.3 %copy.28 = f32[1024]{0:T(1024)} copy(f32[1024]{0:T(1024)} %bitcast.20) | data formatting | bytes 8192
  103.7 0.0 copy-done.5
  103.7 0.6 copy.29
  104.3 1.7 %copy.30 = f32[1024,64]{0,1:T(8,128)} copy(f32[1024,64]{0,1:T(8,128)} %bitcast.16) | data formatting | bytes 524288
  106.0 2.3 %copy.31 = f32[4096,64]{0,1:T(8,128)} copy(f32[4096,64]{0,1:T(8,128)} %bitcast.13) | data formatting | bytes 2097152
Async XLA Ops:
  0.6 0.7 copy-start.3
  0.6 99.2 %copy-start = (bf16[4096,64]{0,1:T(8,128)(2,1)S(1)}, bf16[4096,64]{0,1:T(8,128)(2,1)}, u32[]{:S(2)}) copy-start(bf16[4096,64]{0,1:T(8,128)(2,1)} %param.8) | copy-start | bytes 1572868
  1.3 98.6 %copy-start.1 = (bf16[1024,64]{0,1:T(8,128)(2,1)S(1)}, bf16[1024,64]{0,1:T(8,128)(2,1)}, u32[]{:S(2)}) copy-start(bf16[1024,64]{0,1:T(8,128)(2,1)} %param.7) | copy-start | bytes 393220
  1.3 98.6 %copy-start.2 = (f32[4096]{0:T(1024)S(1)}, f32[4096]{0:T(1024)}, u32[]{:S(2)}) copy-start(f32[4096]{0:T(1024)} %param.10) | copy-start | bytes 49156
  99.9 0.7 copy-start.4
  102.4 1.3 %copy-start.5 = (f32[32,128]{1,0:T(8,128)S(1)}, f32[32,128]{1,0:T(8,128)}, u32[]{:S(2)}) copy-start(f32[32,128]{1,0:T(8,128)} %get-tuple-element.70) | copy-start | bytes 49156

commit v2 on v1

--- a/solution.py
+++ b/solution.py
@@ -18,6 +18,7 @@
 CROSS = UNIT * 2.0 / FEAT
 NORM = UNIT / FEAT
 SIDE = 16
+GAP = 90.0
 MSG = FEAT + 8
 MESH = pl.DeviceIdType.MESH
 F32 = jnp.float32
@@ -54,12 +55,12 @@
 
 
 def sinkhorn_kernel(
-    cap, cfeat, sfeat, cmass, smass, pattern,
+    cap, quick, cfeat_h, sfeat_h, cmass_h, smass_h, pattern_h,
     cpot_out, spot_out, cmap_out, smap_out, flag_out,
-    swap_out, swap_in, side_out, side_in, chh, cht, shh, sht, cross, crosst, spread,
+    cfeat, sfeat, cmass, smass, pattern, swap_out, swap_in, side_out, side_in, chh, cht, shh, sht, cross, crosst, spread,
     blockmap, slot_peak, peak_scr, list_v, list_s, tab_v, tab_s,
     buf_e, buf_d, flag_e, flag_d, msg_c, rcv_c, msg_s, rcv_s, own_c, own_s, pot_s,
-    sem_swap, sem_e, sem_d, sem_map, sem_loc,
+    sem_swap, sem_e, sem_d, sem_map, sem_loc, sem_in, *more,
 ):
     ci = lax.axis_index("cells")
     si = lax.axis_index("spots")
@@ -87,9 +88,23 @@
                 d_peers.append((a + ring(b), (d2 * 2 + core, si), d2))
     d_peers.sort(key=lambda item: -item[0])
 
+    if quick:
+        weight_c, weight_s, bound_c, bound_s, worst = more
+
     barrier = pltpu.get_barrier_semaphore()
     for item in e_peers + d_peers:
         pl.semaphore_signal(barrier, inc=1, device_id=item[1], device_id_type=MESH)
+
+    loads = [
+        pltpu.make_async_copy(src, dst, sem_in.at[k])
+        for k, (src, dst) in enumerate(
+            ((cfeat_h, cfeat), (sfeat_h, sfeat), (cmass_h, cmass), (smass_h, smass), (pattern_h, pattern))
+        )
+    ]
+    for load in loads:
+        load.start()
+    for load in loads:
+        load.wait()
 
     def own_cells(b, _):
         block = cfeat[:, pl.ds(pl.multiple_of(b * BLK, BLK), BLK)]
@@ -168,9 +183,6 @@
     ]
     for copy in copies:
         copy.start()
-    flag_e[eme] = over
-    for _, dev, _, _ in e_peers:
-        send(flag_e.at[eme], flag_e.at[eme], sem_e.at[0, ITERS], sem_e.at[1, ITERS], dev)
 
     cell_log = log2(
         jnp.concatenate(
@@ -196,7 +208,7 @@
     for copy in copies:
         copy.wait()
 
-    step = 4
+    step = 13 if quick else 8
 
     def build(i, _):
         for k in range(step):
@@ -250,39 +262,105 @@
             total = total + jnp.exp2(buf[it, k] - top)
         return top + log2(total)
 
-    def cell_start(it, feats):
-        peak, total = half(crosst, 1, 0, feats)
-        buf_e[it, eme] = joined(peak, total)
+    def cell_send(it, value):
+        buf_e[it, eme] = value
         for _, dev, _, _ in e_peers:
             send(buf_e.at[it, eme], buf_e.at[it, eme], sem_e.at[0, it], sem_e.at[1, it], dev)
-        return peak, total
-
-    def cell_end(it):
+
+    def cell_merge(it):
         wait_for(buf_e.at[it, pl.ds(0, 15)], sem_e.at[1, it])
-        pot = cell_log - merge(buf_e, it, 16)
-        lane_spread(pot, spread)
-        return pot
-
-    def iteration(it, _):
-        cell_start(it, None)
-        cell_end(it)
-        peak, total = half(cross, 0, 1, None)
-        buf_d[it, dme] = joined(peak, total)
+        return merge(buf_e, it, 16)
+
+    def spot_exchange(it, value):
+        buf_d[it, dme] = value
         for _, dev, _ in d_peers:
             send(buf_d.at[it, dme], buf_d.at[it, dme], sem_d.at[0, it], sem_d.at[1, it], dev)
         wait_for(buf_d.at[it, pl.ds(0, 7)], sem_d.at[1, it])
-        lane_spread(spot_log - merge(buf_d, it, 8), spread)
+        return merge(buf_d, it, 8)
+
+    def peaks(i, carry):
+        top_c, top_s = carry
+        for k in range(step):
+            e = i * step + k
+            one = jnp.max(crosst[e], axis=0, keepdims=True)
+            two = jnp.max(cross[e], axis=0, keepdims=True)
+            top_c = jnp.where(rows == list_s[2, e], jnp.maximum(top_c, one), top_c)
+            top_s = jnp.where(rows == list_s[3, e], jnp.maximum(top_s, two), top_s)
+        return top_c, top_s
+
+    def weights(i, _):
+        for k in range(step):
+            e = i * step + k
+            r = within(list_s[0, e], SIDE - 1)
+            c = within(list_s[1, e], SIDE - 1)
+            weight_c[e] = jnp.exp2(crosst[e] - bound_c[pl.ds(r, 1), :])
+            weight_s[e] = jnp.exp2(cross[e] - bound_s[pl.ds(c, 1), :])
         return 0
 
-    lax.fori_loop(0, ITERS - 1, iteration, 0)
-
-    wait_for(flag_e.at[pl.ds(0, 15)], sem_e.at[1, ITERS])
-    over = flag_e[0]
-    for k in range(1, 16):
-        over = jnp.maximum(over, flag_e[k])
-    flag_d[dme] = over
-    for _, dev, _ in d_peers:
-        send(flag_d.at[dme], flag_d.at[dme], sem_d.at[0, ITERS], sem_d.at[1, ITERS], dev)
+    def quick_half(weight, bound, pot, other, own):
+        most = jnp.max(jnp.max(pot, axis=0, keepdims=True), axis=1, keepdims=True)
+        lane_spread(jnp.exp2(pot - most), spread)
+
+        def body(i, total):
+            parts = []
+            for k in range(step):
+                e = i * step + k
+                o = within(list_s[other, e], SIDE - 1)
+                parts.append(
+                    (list_s[own + 2, e], jnp.sum(weight[e] * spread[o], axis=0, keepdims=True))
+                )
+            for at, part in parts:
+                total = total + jnp.where(rows == at, part, 0.0)
+            return total
+
+        total = lax.fori_loop(0, cap // step, body, jnp.zeros((SIDE, BLK), F32))
+        top = bound[...] + most
+        return top, jnp.where(total > 0, top + log2(jnp.maximum(total, 1e-38)), NEG)
+
+    def watch(top, lse):
+        worst[...] = jnp.where(top - lse <= GAP, worst[...], 1.0)
+
+    def quick_spots(it, cell_lse):
+        top, value = quick_half(weight_s, bound_s, cell_log - cell_lse, 0, 1)
+        lse = spot_exchange(it, value)
+        watch(top, lse)
+        return spot_log - lse
+
+    def first_steps():
+        peak, total = half(crosst, 1, 0, None)
+        cell_send(0, joined(peak, total))
+        init = jnp.full((SIDE, BLK), NEG, F32)
+        top_c, top_s = lax.fori_loop(0, cap // step, peaks, (init, init))
+        bound_c[...] = top_c
+        bound_s[...] = top_s
+        worst[...] = jnp.zeros((SIDE, BLK), F32)
+        lax.fori_loop(0, cap // step, weights, 0)
+
+        def iteration(it, lse):
+            pot = quick_spots(it, lse)
+            top, value = quick_half(weight_c, bound_c, pot, 1, 0)
+            cell_send(it + 1, value)
+            lse = cell_merge(it + 1)
+            watch(top, lse)
+            return lse
+
+        lse = lax.fori_loop(0, ITERS - 2, iteration, cell_merge(0))
+        lane_spread(quick_spots(ITERS - 2, lse), spread)
+        return jnp.max(worst[...], axis=0, keepdims=True)
+
+    def first_steps_whole():
+        def iteration(it, _):
+            peak, total = half(crosst, 1, 0, None)
+            cell_send(it, joined(peak, total))
+            lane_spread(cell_log - cell_merge(it), spread)
+            peak, total = half(cross, 0, 1, None)
+            lane_spread(spot_log - spot_exchange(it, joined(peak, total)), spread)
+            return 0
+
+        lax.fori_loop(0, ITERS - 1, iteration, 0)
+        return jnp.zeros((1, BLK), F32)
+
+    over = jnp.maximum(over, first_steps() if quick else first_steps_whole())
 
     def gather_maps(peak, total, msg, transposed):
         peak_scr[...] = peak
@@ -318,18 +396,31 @@
             acc = acc + take(k, pl.ds(0, FEAT)) * scale
         return top + log2(total), acc / total
 
-    peak, total = cell_start(ITERS - 1, shh)
+    peak, total = half(crosst, 1, 0, shh)
+    cell_send(ITERS - 1, joined(peak, total))
+    flag_e[eme] = over
+    for _, dev, _, _ in e_peers:
+        send(flag_e.at[eme], flag_e.at[eme], sem_e.at[0, ITERS], sem_e.at[1, ITERS], dev)
     gather_maps(peak, total, msg_c, False)
     for _, dev, s2, k2 in e_peers:
         send(msg_c.at[k2 * 8 + s2], rcv_c.at[eme], sem_map.at[0], sem_map.at[1], dev)
     rcv_c[eme] = msg_c[core * 8 + si]
-    cell_pot = cell_end(ITERS - 1)
+    cell_pot = cell_log - cell_merge(ITERS - 1)
+    lane_spread(cell_pot, spread)
 
     peak, total = half(cross, 0, 1, chh)
     gather_maps(peak, total, msg_s, True)
     for _, dev, d2 in d_peers:
         send(msg_s.at[pl.ds(d2 * 2, 2)], rcv_s.at[dme], sem_map.at[2], sem_map.at[3], dev)
     rcv_s[dme] = msg_s[pl.ds(dme * 2, 2)]
+
+    wait_for(flag_e.at[pl.ds(0, 15)], sem_e.at[1, ITERS])
+    over = flag_e[0]
+    for k in range(1, 16):
+        over = jnp.maximum(over, flag_e[k])
+    flag_d[dme] = over
+    for _, dev, _ in d_peers:
+        send(flag_d.at[dme], flag_d.at[dme], sem_d.at[0, ITERS], sem_d.at[1, ITERS], dev)
 
     wait_for(rcv_c.at[pl.ds(0, 15)], sem_map.at[1])
     _, block = total_map(lambda k, r: rcv_c[k, r, :], 16)
@@ -380,7 +471,7 @@
     over = flag_d[0]
     for k in range(1, 8):
         over = jnp.maximum(over, flag_d[k])
-    flag_out[...] = over
+    flag_out[0] = jnp.max(over).astype(jnp.int32)
 
     wait_for(cmap_out.at[:, pl.ds(0, 7 * BLK)], sem_map.at[5])
     wait_for(spot_out.at[pl.ds(0, SIDE)], sem_swap.at[5])
@@ -406,12 +497,13 @@
     wait_for(buf_e.at[ITERS - 1, pl.ds(0, 15)], sem_e.at[0, ITERS - 1])
 
 
-def run(cap, collective, cfeat, sfeat, cmass, smass, pattern):
+def run(cap, quick, collective, cfeat, sfeat, cmass, smass, pattern):
     width = 128 if cap <= 128 else 256
     vmem = lambda *shape: pltpu.VMEM(shape, F32)
     half = lambda *shape: pltpu.VMEM(shape, BF16)
     shape = lambda *dims: jax.ShapeDtypeStruct(dims, F32)
     scratch = [
+        half(FEAT, 1024), half(FEAT, 4096), vmem(8, BLK), vmem(32, BLK), pltpu.VMEM((8, 32), jnp.int32),
         vmem(8, FEAT, BLK), vmem(8, FEAT, BLK), vmem(2, 8, BLK), vmem(2, 8, BLK),
         half(SIDE, FEAT, BLK), half(SIDE, BLK, FEAT), half(SIDE, FEAT, BLK), half(SIDE, BLK, FEAT),
         vmem(cap, BLK, BLK), vmem(cap, BLK, BLK), vmem(SIDE, BLK, BLK),
@@ -423,13 +515,15 @@
         vmem(FEAT, BLK), vmem(FEAT, 2 * BLK), vmem(8, 8, BLK),
         pltpu.SemaphoreType.DMA((8,)), pltpu.SemaphoreType.DMA((2, ITERS + 1)),
         pltpu.SemaphoreType.DMA((2, ITERS + 1)), pltpu.SemaphoreType.DMA((10,)),
-        pltpu.SemaphoreType.DMA((2,)),
+        pltpu.SemaphoreType.DMA((2,)), pltpu.SemaphoreType.DMA((5,)),
     ]
+    if quick:
+        scratch += [vmem(cap, BLK, BLK), vmem(cap, BLK, BLK)] + [vmem(SIDE, BLK)] * 3
     return pl.pallas_call(
-        functools.partial(sinkhorn_kernel, cap),
-        out_shape=(shape(8, BLK), shape(32, BLK), shape(FEAT, 1024), shape(FEAT, 4096), shape(8, BLK)),
-        in_specs=[pl.BlockSpec(memory_space=pltpu.VMEM)] * 5,
-        out_specs=tuple([pl.BlockSpec(memory_space=pltpu.VMEM)] * 5),
+        functools.partial(sinkhorn_kernel, cap, quick),
+        out_shape=(shape(8, BLK), shape(32, BLK), shape(FEAT, 1024), shape(FEAT, 4096), jax.ShapeDtypeStruct((1,), jnp.int32)),
+        in_specs=[pl.BlockSpec(memory_space=pltpu.HBM)] * 5,
+        out_specs=tuple([pl.BlockSpec(memory_space=pltpu.VMEM)] * 4 + [pl.BlockSpec(memory_space=pltpu.SMEM)]),
         scratch_shapes=scratch,
         compiler_params=pltpu.CompilerParams(
             collective_id=collective, has_side_effects=True, vmem_limit_bytes=60 * 2**20
@@ -437,11 +531,30 @@
     )(cfeat, sfeat, cmass, smass, pattern)
 
 
+def place_kernel(*refs):
+    srcs, dsts, sems = refs[:4], refs[4:8], refs[8]
+    copies = [pltpu.make_async_copy(s, d, sems.at[k]) for k, (s, d) in enumerate(zip(srcs, dsts))]
+    for copy in copies:
+        copy.start()
+    for copy in copies:
+        copy.wait()
+
+
+def place(*arrays):
+    return pl.pallas_call(
+        place_kernel,
+        out_shape=tuple(jax.ShapeDtypeStruct(a.shape, a.dtype) for a in arrays),
+        in_specs=[pl.BlockSpec(memory_space=pl.ANY)] * 4,
+        out_specs=tuple([pl.BlockSpec(memory_space=pl.ANY)] * 4),
+        scratch_shapes=[pltpu.SemaphoreType.DMA((4,))],
+    )(*arrays)
+
+
 def per_device(cell_feat, spot_feat, cell_mass, spot_mass, block_pattern):
     args = (cell_feat.T, spot_feat.T, cell_mass.reshape(8, BLK), spot_mass.reshape(32, BLK), block_pattern)
-    outs = run(56, 0, *args)
-    cpot, spot, cmap, smap, _ = lax.while_loop(
-        lambda now: now[4][0, 0] > 0, lambda now: run(SIDE * SIDE, 1, *args), outs
+    outs = run(52, True, 0, *args)
+    cpot, spot, cmap, smap = lax.cond(
+        outs[4][0] > 0, lambda now: place(*run(SIDE * SIDE, False, 1, *args)[:4]), lambda now: place(*now[:4]), outs
     )
     return cpot.reshape(1024), spot.reshape(4096), cmap.T, smap.T
 

time: 109 us -> 270 us (2.48)
  Pallas kernels: 98.5 us -> 268 us
  local copies, waits for them, and re-layouts: 8.35 us -> 0.69 us
    pallas_call x1 -> x3, Pallas kernels: 98.5 us -> 268 us  [the longest x2 227 us: run(): pl.pallas_call(functools.partial(sinkhorn_kernel, cap, quick), out_shape=...]
    unnamed x16 -> x10, local copies, waits for them, and re-layouts: 7.16 us -> 0.69 us
where the time goes in v2:
time: 270 us
  Pallas kernels  268 us (99%)
    pallas_call x2, Pallas kernels, run(): pl.pallas_call(functools.partial(sinkhorn_kernel, cap, quick), out_shape=...  227 us
    pallas_call x1, Pallas kernels, place(): pl.pallas_call(place_kernel, out_shape=tuple((jax.ShapeDtypeStruct(a.shap...  41.5 us

profile of v2, /device:TPU:1, one launch (start us, length us, event | category | flops | bytes accessed | tf_op | source)
XLA Modules:
  0.0 270.1 jit_solution(4293340454148972534)
XLA Ops:
  0.6 0.0 copy-start.3
  0.6 0.0 copy-start.4
  0.7 0.0 copy-start
  0.7 0.7 copy-done.3
  1.3 0.0 copy-done.4
  1.3 0.0 copy-start.1
  1.3 0.0 copy-start.2
  1.3 88.9 %shard_map.84 = (f32[8,128]{1,0:T(8,128)S(1)}, f32[32,128]{1,0:T(8,128)S(1)}, f32[64,1024]{1,0:T(8,128)S(1)}, f32[64,4096]{1,0:T(8,128)S(1)}, s32[1]{0:T(128)}) custom-call(bf16[64,1024]{1,0:T(8,128)(2,1)} %bitcast.11, bf16[64,4096]{1,0:T(8,128)(2,1)} %bitcast.9, f32[8,128]{1,0:T(8,128)S(1)} %bitcast.15, f32[32,128]{1,0:T(8,128)} %bitcast.13, ...), custom_call_target="tpu_custom_call" | custom-call | tf_op jit(solution)/shard_map/pallas_call | solution.py:522
  90.8 0.0 copy-done
  90.9 0.0 copy-done.1
  90.9 0.0 copy-done.2
  90.9 179.2 %conditional.1 = ((f32[8,128]{1,0:T(8,128)}, f32[32,128]{1,0:T(8,128)}, f32[64,1024]{1,0:T(8,128)}, f32[64,4096]{1,0:T(8,128)})) conditional(s32[]{:T(128)} %bitcast.4, (f32[8,128]{1,0:T(8,128)S(1)}, f32[32,128]{1,0:T(8,128)S(1)}, f32[64,1024]{1,0:T(8,128)S(1)}, f32[64,4096]{1,0:T(8,128)S(1)}) %tuple.25, (bf16[64,1024]{1,0:T(8,128)(2,1)S(1)}, ...), branch_computations={%region_0.0_spmd.clone, %region_1.0_spmd.clone} | conditional | bytes 8 | solution.py:556
  90.9 137.7 %branch_1_fun.4 = (f32[8,128]{1,0:T(8,128)}, f32[32,128]{1,0:T(8,128)}, f32[64,1024]{1,0:T(8,128)}, f32[64,4096]{1,0:T(8,128)}, s32[1]{0:T(128)}) custom-call(bf16[64,1024]{1,0:T(8,128)(2,1)S(1)} %get-tuple-element.92.cfeat_h, bf16[64,4096]{1,0:T(8,128)(2,1)S(1)} %get-tuple-element.93.sfeat_h, f32[8,128]{1,0:T(8,128)S(1)} %get-tuple-element.94.cmass_h, ...), custom_call_target="tpu_custom_call" | custom-call | tf_op jit(solution)/shard_map/cond/branch_1_fun/pallas_call | solution.py:522
  228.6 41.5 %branch_1_fun.5 = (f32[8,128]{1,0:T(8,128)}, f32[32,128]{1,0:T(8,128)}, f32[64,1024]{1,0:T(8,128)}, f32[64,4096]{1,0:T(8,128)}) custom-call(f32[8,128]{1,0:T(8,128)} %get-tuple-element.97.refs_0_, f32[32,128]{1,0:T(8,128)} %get-tuple-element.98.refs_1_, f32[64,1024]{1,0:T(8,128)} %get-tuple-element.99.refs_2_, f32[64,4096]{1,0:T(8,128)} %get-tuple-element.100.refs_3_), custom_call_target="tpu_custom_call" | custom-call | tf_op jit(solution)/shard_map/cond/branch_1_fun/pallas_call | solution.py:544
Async XLA Ops:
  0.6 0.7 copy-start.3
  0.6 0.7 copy-start.4
  0.7 90.2 %copy-start = (bf16[4096,64]{0,1:T(8,128)(2,1)S(1)}, bf16[4096,64]{0,1:T(8,128)(2,1)}, u32[]{:S(2)}) copy-start(bf16[4096,64]{0,1:T(8,128)(2,1)} %param.8) | copy-start | bytes 1572868
  1.3 89.5 %copy-start.1 = (bf16[1024,64]{0,1:T(8,128)(2,1)S(1)}, bf16[1024,64]{0,1:T(8,128)(2,1)}, u32[]{:S(2)}) copy-start(bf16[1024,64]{0,1:T(8,128)(2,1)} %param.7) | copy-start | bytes 393220
  1.3 89.5 %copy-start.2 = (f32[4096]{0:T(1024)S(1)}, f32[4096]{0:T(1024)}, u32[]{:S(2)}) copy-start(f32[4096]{0:T(1024)} %param.10) | copy-start | bytes 49156

commit v3 on v2

--- a/solution.py
+++ b/solution.py
@@ -18,7 +18,9 @@
 CROSS = UNIT * 2.0 / FEAT
 NORM = UNIT / FEAT
 SIDE = 16
+FIRST = 56
 GAP = 90.0
+DEEP = FEAT + 16
 MSG = FEAT + 8
 MESH = pl.DeviceIdType.MESH
 F32 = jnp.float32
@@ -48,10 +50,43 @@
 
 
 def lane_spread(pot, out):
-    full = jnp.concatenate([pot, jnp.zeros((BLK - SIDE, BLK), F32)], axis=0)
-    turned = jnp.transpose(full)
     for b in range(SIDE):
-        out[b] = jnp.broadcast_to(turned[:, b : b + 1], (BLK, BLK))
+        out[b] = jnp.transpose(jnp.broadcast_to(pot[b : b + 1], (BLK, BLK)))
+
+
+def block_list(allowed, lane0, cols, width):
+    rows = allowed.shape[0]
+    upto = (
+        lax.broadcasted_iota(jnp.int32, (BLK, BLK), 0)
+        < lax.broadcasted_iota(jnp.int32, (BLK, BLK), 1)
+    ).astype(BF16)
+    inside = jnp.dot(allowed.astype(BF16), upto, preferred_element_type=F32)
+    per_row = jnp.broadcast_to(jnp.sum(allowed, axis=1, keepdims=True), (rows, BLK))
+    below = lax.broadcasted_iota(jnp.int32, (rows, BLK), 0)
+    before = jnp.zeros((rows, BLK), F32)
+    for r in range(rows - 1):
+        before = before + jnp.where(below > r, per_row[r : r + 1], 0.0)
+    place = jnp.where(allowed > 0, before + inside, -1.0)
+    count = jnp.sum(jnp.sum(allowed, axis=1, keepdims=True), axis=0, keepdims=True)
+    pairs = rows * cols
+    wide_place = jnp.broadcast_to(place[:, None, :], (rows, cols, BLK)).reshape(pairs, BLK)
+    pair = lax.broadcasted_iota(jnp.int32, (pairs, BLK), 0)
+    pair_lane = lax.broadcasted_iota(jnp.int32, (pairs, BLK), 1)
+    chosen = pair_lane == lane0 + pair % cols
+    slot_of = jnp.sum(jnp.where(chosen, wide_place, 0.0), axis=1, keepdims=True)
+    hot = slot_of == lax.broadcasted_iota(jnp.int32, (pairs, width), 1).astype(F32)
+    kind = lax.broadcasted_iota(jnp.int32, (8, pairs), 0)
+    which = lax.broadcasted_iota(jnp.int32, (8, pairs), 1)
+    facts = jnp.where(kind == 0, which // cols, jnp.where(kind == 1, which % cols, 1))
+    lists = jnp.dot(
+        facts.astype(F32).astype(BF16), hot.astype(F32).astype(BF16), preferred_element_type=F32
+    )
+    none = 99.0 * (1.0 - lists[2:3])
+    kind = lax.broadcasted_iota(jnp.int32, (8, width), 0)
+    lists = jnp.where(kind >= 2, 0.0, lists) + jnp.where(
+        kind == 2, lists[0:1] + none, jnp.where(kind == 3, lists[1:2] + none, 0.0)
+    )
+    return lists, place, count
 
 
 def sinkhorn_kernel(
@@ -89,7 +124,7 @@
     d_peers.sort(key=lambda item: -item[0])
 
     if quick:
-        weight_c, weight_s, bound_c, bound_s, worst = more
+        weight_c, weight_s, bound_c, bound_s, worst, chx, list0_v, list0_s, buf_0 = more
 
     barrier = pltpu.get_barrier_semaphore()
     for item in e_peers + d_peers:
@@ -98,38 +133,105 @@
     loads = [
         pltpu.make_async_copy(src, dst, sem_in.at[k])
         for k, (src, dst) in enumerate(
-            ((cfeat_h, cfeat), (sfeat_h, sfeat), (cmass_h, cmass), (smass_h, smass), (pattern_h, pattern))
+            ((pattern_h, pattern), (cfeat_h, cfeat), (sfeat_h, sfeat), (cmass_h, cmass), (smass_h, smass))
         )
     ]
     for load in loads:
         load.start()
-    for load in loads:
-        load.wait()
-
-    def own_cells(b, _):
-        block = cfeat[:, pl.ds(pl.multiple_of(b * BLK, BLK), BLK)]
-        wide = block.astype(F32)
-        swap_out[b] = wide
-        chh[core * 8 + b] = block
-        cht[core * 8 + b] = jnp.transpose(wide).astype(BF16)
+    loads[0].wait()
+    pattern_own = (pattern[...] > 0).astype(F32)
+    side_out[1] = jnp.concatenate([pattern_own, jnp.zeros((8, BLK - 32), F32)], axis=1)
+    if quick:
+        lists, _, count_0 = block_list(side_out[1], 0, 2 * SIDE, list0_v.shape[1])
+        list0_v[...] = lists.astype(jnp.int32)
+        copy_0 = pltpu.make_async_copy(list0_v, list0_s, sem_loc.at[2])
+        copy_0.start()
+    loads[1].wait()
+    below = lax.broadcasted_iota(jnp.int32, (DEEP - FEAT, BLK), 0)
+
+    def cells_turned(b, wide):
+        cht[b] = jnp.transpose(wide).astype(BF16)
+
+    def own_cells(i, _):
+        for k in range(4):
+            b = i * 4 + k
+            block = cfeat[:, pl.ds(pl.multiple_of(b * BLK, BLK), BLK)]
+            wide = block.astype(F32)
+            swap_out[b] = wide
+            chh[core * 8 + b] = block
+            if quick:
+                ones = jnp.where(below < 3, 1.0, 0.0).astype(BF16)
+                chx[b] = jnp.concatenate([block, ones], axis=0)
+            else:
+                cells_turned(core * 8 + b, wide)
         return 0
 
-    lax.fori_loop(0, 8, own_cells, 0)
-
-    def own_spots(b, norms):
-        block = sfeat[:, pl.ds(pl.multiple_of((core * SIDE + b) * BLK, BLK), BLK)]
-        wide = block.astype(F32)
-        shh[b] = block
-        sht[b] = jnp.transpose(wide).astype(BF16)
-        here = lax.broadcasted_iota(jnp.int32, (SIDE, BLK), 0) == b
-        return jnp.where(here, jnp.sum(wide * wide, axis=0, keepdims=True) * NORM, norms)
-
-    spot_norm = lax.fori_loop(0, SIDE, own_spots, jnp.zeros((SIDE, BLK), F32))
-    pattern_own = (pattern[...] > 0).astype(F32)
+    lax.fori_loop(0, 2, own_cells, 0)
+    loads[2].wait()
+
+    spots = 2 * SIDE if quick else SIDE
+    offset = 0 if quick else core * SIDE
+    mid = core * SIDE if quick else 0
+
+    def own_spots(i, norms):
+        for k in range(4):
+            b = i * 4 + k
+            block = sfeat[:, pl.ds(pl.multiple_of((offset + b) * BLK, BLK), BLK)]
+            wide = block.astype(F32)
+            norm = jnp.sum(wide * wide, axis=0, keepdims=True)
+            shh[b] = block
+            if quick:
+                rest = norm * -0.5
+                parts = jnp.zeros((DEEP - FEAT, BLK), F32)
+                for n in range(3):
+                    part = rest.astype(BF16).astype(F32)
+                    parts = jnp.where(below == n, part, parts)
+                    rest = rest - part
+                wide = jnp.concatenate([wide, parts], axis=0)
+            sht[b] = jnp.transpose(wide).astype(BF16)
+            here = lax.broadcasted_iota(jnp.int32, (SIDE, BLK), 0) == b - mid
+            norms = jnp.where(here, norm * NORM, norms)
+        return norms
+
+    spot_norm = lax.fori_loop(0, spots // 4, own_spots, jnp.zeros((SIDE, BLK), F32))
+
+    def first_half():
+        copy_0.wait()
+        rows8 = lax.broadcasted_iota(jnp.int32, (8, BLK), 0)
+        step = 14
+
+        def body(i, carry):
+            peak, total = carry
+            parts = []
+            for k in range(step):
+                e = i * step + k
+                r = within(list0_s[0, e], 7)
+                c = within(list0_s[1, e], 2 * SIDE - 1)
+                v = jnp.dot(sht[c], chx[r], preferred_element_type=F32) * CROSS
+                top = jnp.max(v, axis=0, keepdims=True)
+                part = jnp.sum(jnp.exp2(v - top), axis=0, keepdims=True)
+                parts.append((list0_s[2, e], top, part))
+            for at, top, part in parts:
+                new = jnp.where(rows8 == at, jnp.maximum(peak, top), peak)
+                total = total * jnp.exp2(peak - new) + jnp.where(
+                    rows8 == at, part * jnp.exp2(top - new), 0.0
+                )
+                peak = new
+            return peak, total
+
+        init = (jnp.full((8, BLK), NEG, F32), jnp.zeros((8, BLK), F32))
+        peak, total = lax.fori_loop(0, FIRST // step, body, init)
+        buf_0[eme] = jnp.where(total > 0, peak + log2(jnp.maximum(total, 1e-30)), NEG)
+        return jnp.where(count_0 > FIRST, 1.0, 0.0)
+
+    over_0 = first_half() if quick else None
+    pl.semaphore_wait(barrier, len(e_peers) + len(d_peers))
+    loads[3].wait()
+    loads[4].wait()
     side_out[0] = cmass[...]
-    side_out[1] = jnp.concatenate([pattern_own, jnp.zeros((8, BLK - 32), F32)], axis=1)
-
-    pl.semaphore_wait(barrier, len(e_peers) + len(d_peers))
+    if quick:
+        for _, dev, _, _ in e_peers:
+            send(buf_0.at[eme], buf_0.at[eme], sem_e.at[0, 0], sem_e.at[1, 0], dev)
 
     send(side_out, side_in, sem_swap.at[0], sem_swap.at[1], partner)
     send(swap_out, swap_in, sem_swap.at[2], sem_swap.at[3], partner)
@@ -142,39 +244,8 @@
         [jnp.where(first, mine, theirs), jnp.where(first, theirs, mine)], axis=0
     )
     both = jnp.where((lane >= core * SIDE) & (lane < core * SIDE + SIDE), both, 0.0)
-    upto = (
-        lax.broadcasted_iota(jnp.int32, (BLK, BLK), 0)
-        < lax.broadcasted_iota(jnp.int32, (BLK, BLK), 1)
-    ).astype(BF16)
-    inside = jnp.dot(both.astype(BF16), upto, preferred_element_type=F32)
-    per_row = jnp.broadcast_to(jnp.sum(both, axis=1, keepdims=True), (SIDE, BLK))
-    earlier = (
-        lax.broadcasted_iota(jnp.int32, (SIDE, SIDE), 1)
-        < lax.broadcasted_iota(jnp.int32, (SIDE, SIDE), 0)
-    ).astype(BF16)
-    before = jnp.dot(earlier, per_row.astype(BF16), preferred_element_type=F32)
-    place = jnp.where(both > 0, before + inside, -1.0)
-    count = jnp.sum(jnp.sum(both, axis=1, keepdims=True), axis=0, keepdims=True)
+    lists, place, count = block_list(both, core * SIDE, SIDE, list_v.shape[1])
     over = jnp.broadcast_to(jnp.where(count > cap, 1.0, 0.0), (8, BLK))
-    width = list_v.shape[1]
-    pairs = SIDE * SIDE
-    wide_place = jnp.broadcast_to(place[:, None, :], (SIDE, SIDE, BLK)).reshape(pairs, BLK)
-    pair = lax.broadcasted_iota(jnp.int32, (pairs, BLK), 0)
-    pair_lane = lax.broadcasted_iota(jnp.int32, (pairs, BLK), 1)
-    chosen = pair_lane == core * SIDE + pair % SIDE
-    slot_of = jnp.sum(jnp.where(chosen, wide_place, 0.0), axis=1, keepdims=True)
-    hot = slot_of == lax.broadcasted_iota(jnp.int32, (pairs, width), 1).astype(F32)
-    kind = lax.broadcasted_iota(jnp.int32, (8, pairs), 0)
-    which = lax.broadcasted_iota(jnp.int32, (8, pairs), 1)
-    facts = jnp.where(kind == 0, which // SIDE, jnp.where(kind == 1, which % SIDE, 1))
-    lists = jnp.dot(
-        facts.astype(F32).astype(BF16), hot.astype(F32).astype(BF16), preferred_element_type=F32
-    )
-    none = 99.0 * (1.0 - lists[2:3])
-    kind = lax.broadcasted_iota(jnp.int32, (8, width), 0)
-    lists = jnp.where(kind >= 2, 0.0, lists) + jnp.where(
-        kind == 2, lists[0:1] + none, jnp.where(kind == 3, lists[1:2] + none, 0.0)
-    )
     list_v[...] = lists.astype(jnp.int32)
     tab_v[...] = jnp.where((place < 0) | (place >= cap), float(cap), place).astype(jnp.int32)
     copies = [
@@ -195,31 +266,41 @@
     )
     spot_log = log2(smass[pl.ds(pl.multiple_of(core * SIDE, SIDE), SIDE), :])
 
-    lane_spread(-spot_norm, spread)
+    if not quick:
+        lane_spread(-spot_norm, spread)
     wait_for(swap_in, sem_swap.at[3])
 
-    def other_cells(b, _):
-        wide = swap_in[b]
-        chh[(1 - core) * 8 + b] = wide.astype(BF16)
-        cht[(1 - core) * 8 + b] = jnp.transpose(wide).astype(BF16)
+    def other_cells(i, _):
+        for k in range(4):
+            b = i * 4 + k
+            wide = swap_in[b]
+            chh[(1 - core) * 8 + b] = wide.astype(BF16)
+            cells_turned((1 - core) * 8 + b, wide)
+            if quick:
+                cells_turned(core * 8 + b, swap_out[b])
         return 0
 
-    lax.fori_loop(0, 8, other_cells, 0)
+    lax.fori_loop(0, 2, other_cells, 0)
     for copy in copies:
         copy.wait()
 
-    step = 13 if quick else 8
-
-    def build(i, _):
-        for k in range(step):
-            e = i * step + k
-            r = within(list_s[0, e], SIDE - 1)
-            c = within(list_s[1, e], SIDE - 1)
-            cross[e] = jnp.dot(cht[r], shh[c], preferred_element_type=F32) * CROSS
-            crosst[e] = jnp.dot(sht[c], chh[r], preferred_element_type=F32) * CROSS
-        return 0
-
-    lax.fori_loop(0, cap // step, build, 0)
+    step = 26 if quick else 8
+
+    def build(with_cross, with_crosst):
+        def some(i, _):
+            for k in range(step):
+                e = i * step + k
+                r = within(list_s[0, e], SIDE - 1)
+                c = within(list_s[1, e], SIDE - 1)
+                if with_cross:
+                    cross[e] = jnp.dot(cht[r], shh[mid + c], preferred_element_type=F32) * CROSS
+                if with_crosst:
+                    crosst[e] = jnp.dot(sht[mid + c, :, :FEAT], chh[r], preferred_element_type=F32) * CROSS
+            return 0
+
+        lax.fori_loop(0, cap // step, some, 0)
+
+    build(True, not quick)
 
     rows = lax.broadcasted_iota(jnp.int32, (SIDE, BLK), 0)
 
@@ -237,7 +318,7 @@
                 if feats is not None:
                     slot_peak[e] = top
                     blockmap[e] = jnp.dot(
-                        feats[o], p.astype(BF16), preferred_element_type=F32
+                        feats(o), p.astype(BF16), preferred_element_type=F32
                     )
             for at, top, part in parts:
                 new = jnp.where(rows == at, jnp.maximum(peak, top), peak)
@@ -253,14 +334,17 @@
     def joined(peak, total):
         return jnp.where(total > 0, peak + log2(jnp.maximum(total, 1e-30)), NEG)
 
-    def merge(buf, it, n):
-        top = buf[it, 0]
-        for k in range(1, n):
-            top = jnp.maximum(top, buf[it, k])
-        total = jnp.exp2(buf[it, 0] - top)
-        for k in range(1, n):
-            total = total + jnp.exp2(buf[it, k] - top)
-        return top + log2(total)
+    def merge(parts):
+        top = parts[0]
+        for part in parts[1:]:
+            top = jnp.maximum(top, part)
+        total = jnp.exp2(parts[0] - top)
+        for part in parts[1:]:
+            total = total + jnp.exp2(part - top)
+        return top, total
+
+    def settled(merged):
+        return merged[0] + log2(merged[1])
 
     def cell_send(it, value):
         buf_e[it, eme] = value
@@ -269,14 +353,16 @@
 
     def cell_merge(it):
         wait_for(buf_e.at[it, pl.ds(0, 15)], sem_e.at[1, it])
-        return merge(buf_e, it, 16)
-
-    def spot_exchange(it, value):
+        return merge([buf_e[it, k] for k in range(16)])
+
+    def spot_send(it, value):
         buf_d[it, dme] = value
         for _, dev, _ in d_peers:
             send(buf_d.at[it, dme], buf_d.at[it, dme], sem_d.at[0, it], sem_d.at[1, it], dev)
+
+    def spot_merge(it):
         wait_for(buf_d.at[it, pl.ds(0, 7)], sem_d.at[1, it])
-        return merge(buf_d, it, 8)
+        return merge([buf_d[it, k] for k in range(8)])
 
     def peaks(i, carry):
         top_c, top_s = carry
@@ -297,9 +383,11 @@
             weight_s[e] = jnp.exp2(cross[e] - bound_s[pl.ds(c, 1), :])
         return 0
 
-    def quick_half(weight, bound, pot, other, own):
-        most = jnp.max(jnp.max(pot, axis=0, keepdims=True), axis=1, keepdims=True)
-        lane_spread(jnp.exp2(pot - most), spread)
+    def largest(pot):
+        return jnp.max(jnp.max(pot, axis=0, keepdims=True), axis=1, keepdims=True)
+
+    def quick_half(weight, bound, log_mass, merged, shift, other, own):
+        lane_spread(jnp.exp2(log_mass - merged[0] - shift) / merged[1], spread)
 
         def body(i, total):
             parts = []
@@ -314,47 +402,59 @@
             return total
 
         total = lax.fori_loop(0, cap // step, body, jnp.zeros((SIDE, BLK), F32))
-        top = bound[...] + most
+        top = bound[...] + shift
         return top, jnp.where(total > 0, top + log2(jnp.maximum(total, 1e-38)), NEG)
 
     def watch(top, lse):
-        worst[...] = jnp.where(top - lse <= GAP, worst[...], 1.0)
-
-    def quick_spots(it, cell_lse):
-        top, value = quick_half(weight_s, bound_s, cell_log - cell_lse, 0, 1)
-        lse = spot_exchange(it, value)
-        watch(top, lse)
-        return spot_log - lse
+        near = (top - lse <= GAP) & (lse - top <= 1.5 * GAP) | (top < 0.5 * NEG) & (lse > 0.5 * NEG)
+        worst[...] = jnp.where(near, worst[...], 1.0)
 
     def first_steps():
-        peak, total = half(crosst, 1, 0, None)
-        cell_send(0, joined(peak, total))
+        wait_for(buf_0.at[pl.ds(0, 15)], sem_e.at[1, 0])
+        cells = jnp.concatenate(
+            [settled(merge([buf_0[2 * k + c] for k in range(8)])) for c in range(2)], axis=0
+        )
+        cells = cell_log - cells
+        lane_spread(cells, spread)
+        peak, total = half(cross, 0, 1, None)
+        spot_send(0, joined(peak, total))
+        build(False, True)
         init = jnp.full((SIDE, BLK), NEG, F32)
         top_c, top_s = lax.fori_loop(0, cap // step, peaks, (init, init))
         bound_c[...] = top_c
         bound_s[...] = top_s
         worst[...] = jnp.zeros((SIDE, BLK), F32)
         lax.fori_loop(0, cap // step, weights, 0)
-
-        def iteration(it, lse):
-            pot = quick_spots(it, lse)
-            top, value = quick_half(weight_c, bound_c, pot, 1, 0)
-            cell_send(it + 1, value)
-            lse = cell_merge(it + 1)
+        spots = spot_merge(0)
+
+        def iteration(it, carry):
+            spots, shift_c, shift_s = carry
+            top, value = quick_half(weight_c, bound_c, spot_log, spots, shift_s, 1, 0)
+            cell_send(it, value)
+            cells = cell_merge(it)
+            top_s, value = quick_half(weight_s, bound_s, cell_log, cells, shift_c, 0, 1)
+            spot_send(it, value)
+            lse = settled(cells)
             watch(top, lse)
-            return lse
-
-        lse = lax.fori_loop(0, ITERS - 2, iteration, cell_merge(0))
-        lane_spread(quick_spots(ITERS - 2, lse), spread)
-        return jnp.max(worst[...], axis=0, keepdims=True)
+            shift_c = largest(cell_log - lse)
+            spots = spot_merge(it)
+            lse = settled(spots)
+            watch(top_s, lse)
+            return spots, shift_c, largest(spot_log - lse)
+
+        carry = (spots, largest(cells), largest(spot_log - settled(spots)))
+        spots, _, _ = lax.fori_loop(1, ITERS - 1, iteration, carry)
+        lane_spread(spot_log - settled(spots), spread)
+        return jnp.maximum(over_0, jnp.max(worst[...], axis=0, keepdims=True))
 
     def first_steps_whole():
         def iteration(it, _):
             peak, total = half(crosst, 1, 0, None)
             cell_send(it, joined(peak, total))
-            lane_spread(cell_log - cell_merge(it), spread)
+            lane_spread(cell_log - settled(cell_merge(it)), spread)
             peak, total = half(cross, 0, 1, None)
-            lane_spread(spot_log - spot_exchange(it, joined(peak, total)), spread)
+            spot_send(it, joined(peak, total))
+            lane_spread(spot_log - settled(spot_merge(it)), spread)
             return 0
 
         lax.fori_loop(0, ITERS - 1, iteration, 0)
@@ -396,7 +496,7 @@
             acc = acc + take(k, pl.ds(0, FEAT)) * scale
         return top + log2(total), acc / total
 
-    peak, total = half(crosst, 1, 0, shh)
+    peak, total = half(crosst, 1, 0, lambda o: shh[mid + o])
     cell_send(ITERS - 1, joined(peak, total))
     flag_e[eme] = over
     for _, dev, _, _ in e_peers:
@@ -405,10 +505,10 @@
     for _, dev, s2, k2 in e_peers:
         send(msg_c.at[k2 * 8 + s2], rcv_c.at[eme], sem_map.at[0], sem_map.at[1], dev)
     rcv_c[eme] = msg_c[core * 8 + si]
-    cell_pot = cell_log - cell_merge(ITERS - 1)
+    cell_pot = cell_log - settled(cell_merge(ITERS - 1))
     lane_spread(cell_pot, spread)
 
-    peak, total = half(cross, 0, 1, chh)
+    peak, total = half(cross, 0, 1, lambda o: chh[o])
     gather_maps(peak, total, msg_s, True)
     for _, dev, d2 in d_peers:
         send(msg_s.at[pl.ds(d2 * 2, 2)], rcv_s.at[dme], sem_map.at[2], sem_map.at[3], dev)
@@ -493,19 +593,23 @@
         wait_for(buf_d.at[it, pl.ds(0, 7)], sem_d.at[0, it])
         return 0
 
-    lax.fori_loop(0, ITERS - 1, sent, 0)
+    if quick:
+        wait_for(buf_0.at[pl.ds(0, 15)], sem_e.at[0, 0])
+        wait_for(buf_d.at[0, pl.ds(0, 7)], sem_d.at[0, 0])
+    lax.fori_loop(1 if quick else 0, ITERS - 1, sent, 0)
     wait_for(buf_e.at[ITERS - 1, pl.ds(0, 15)], sem_e.at[0, ITERS - 1])
 
 
 def run(cap, quick, collective, cfeat, sfeat, cmass, smass, pattern):
     width = 128 if cap <= 128 else 256
+    spots = 2 * SIDE if quick else SIDE
     vmem = lambda *shape: pltpu.VMEM(shape, F32)
     half = lambda *shape: pltpu.VMEM(shape, BF16)
     shape = lambda *dims: jax.ShapeDtypeStruct(dims, F32)
     scratch = [
         half(FEAT, 1024), half(FEAT, 4096), vmem(8, BLK), vmem(32, BLK), pltpu.VMEM((8, 32), jnp.int32),
         vmem(8, FEAT, BLK), vmem(8, FEAT, BLK), vmem(2, 8, BLK), vmem(2, 8, BLK),
-        half(SIDE, FEAT, BLK), half(SIDE, BLK, FEAT), half(SIDE, FEAT, BLK), half(SIDE, BLK, FEAT),
+        half(SIDE, FEAT, BLK), half(SIDE, BLK, FEAT), half(spots, FEAT, BLK), half(spots, BLK, DEEP if quick else FEAT),
         vmem(cap, BLK, BLK), vmem(cap, BLK, BLK), vmem(SIDE, BLK, BLK),
         vmem(cap + 1, FEAT, BLK), vmem(cap + 1, 1, BLK), vmem(SIDE, BLK),
         pltpu.VMEM((8, width), jnp.int32), pltpu.SMEM((8, width), jnp.int32),
@@ -515,10 +619,14 @@
         vmem(FEAT, BLK), vmem(FEAT, 2 * BLK), vmem(8, 8, BLK),
         pltpu.SemaphoreType.DMA((8,)), pltpu.SemaphoreType.DMA((2, ITERS + 1)),
         pltpu.SemaphoreType.DMA((2, ITERS + 1)), pltpu.SemaphoreType.DMA((10,)),
-        pltpu.SemaphoreType.DMA((2,)), pltpu.SemaphoreType.DMA((5,)),
+        pltpu.SemaphoreType.DMA((3,)), pltpu.SemaphoreType.DMA((5,)),
     ]
     if quick:
-        scratch += [vmem(cap, BLK, BLK), vmem(cap, BLK, BLK)] + [vmem(SIDE, BLK)] * 3
+        scratch += [
+            vmem(cap, BLK, BLK), vmem(cap, BLK, BLK), vmem(SIDE, BLK), vmem(SIDE, BLK), vmem(SIDE, BLK),
+            half(8, DEEP, BLK), pltpu.VMEM((8, BLK), jnp.int32), pltpu.SMEM((8, BLK), jnp.int32),
+            vmem(16, 8, BLK),
+        ]
     return pl.pallas_call(
         functools.partial(sinkhorn_kernel, cap, quick),
         out_shape=(shape(8, BLK), shape(32, BLK), shape(FEAT, 1024), shape(FEAT, 4096), jax.ShapeDtypeStruct((1,), jnp.int32)),

time: 270 us -> 262 us (0.970)
  Pallas kernels: 268 us -> 259 us
    pallas_call x2, Pallas kernels: 227 us -> 218 us  [run(): pl.pallas_call(functools.partial(sinkhorn_kernel, cap, quick), out_shape=...]
where the time goes in v3:
time: 262 us; the launch traced here: 261 us
  Pallas kernels  259 us (99%)
    pallas_call x2, Pallas kernels, run(): pl.pallas_call(functools.partial(sinkhorn_kernel, cap, quick), out_shape=...  218 us
    pallas_call x1, Pallas kernels, place(): pl.pallas_call(place_kernel, out_shape=tuple((jax.ShapeDtypeStruct(a.shap...  41.5 us

profile of v3, /device:TPU:1, one launch (start us, length us, event | category | flops | bytes accessed | tf_op | source)
XLA Modules:
  0.0 261.4 jit_solution(2606997218415830797)
XLA Ops:
  0.6 0.0 copy-start.3
  0.6 0.0 copy-start.4
  0.7 0.0 copy-start
  0.7 0.7 copy-done.3
  1.3 0.0 copy-done.4
  1.3 0.0 copy-start.1
  1.3 0.0 copy-start.2
  1.3 81.8 %shard_map.84 = (f32[8,128]{1,0:T(8,128)S(1)}, f32[32,128]{1,0:T(8,128)S(1)}, f32[64,1024]{1,0:T(8,128)S(1)}, f32[64,4096]{1,0:T(8,128)S(1)}, s32[1]{0:T(128)}) custom-call(bf16[64,1024]{1,0:T(8,128)(2,1)} %bitcast.11, bf16[64,4096]{1,0:T(8,128)(2,1)} %bitcast.9, f32[8,128]{1,0:T(8,128)S(1)} %bitcast.15, f32[32,128]{1,0:T(8,128)} %bitcast.13, ...), custom_call_target="tpu_custom_call" | custom-call | tf_op jit(solution)/shard_map/pallas_call | solution.py:630
  83.8 0.0 copy-done
  83.8 0.0 copy-done.1
  83.8 0.0 copy-done.2
  83.8 177.5 %conditional.1 = ((f32[8,128]{1,0:T(8,128)}, f32[32,128]{1,0:T(8,128)}, f32[64,1024]{1,0:T(8,128)}, f32[64,4096]{1,0:T(8,128)})) conditional(s32[]{:T(128)} %bitcast.4, (f32[8,128]{1,0:T(8,128)S(1)}, f32[32,128]{1,0:T(8,128)S(1)}, f32[64,1024]{1,0:T(8,128)S(1)}, f32[64,4096]{1,0:T(8,128)S(1)}) %tuple.25, (bf16[64,1024]{1,0:T(8,128)(2,1)S(1)}, ...), branch_computations={%region_0.0_spmd.clone, %region_1.0_spmd.clone} | conditional | bytes 8 | solution.py:664
  83.9 136.1 %branch_1_fun.4 = (f32[8,128]{1,0:T(8,128)}, f32[32,128]{1,0:T(8,128)}, f32[64,1024]{1,0:T(8,128)}, f32[64,4096]{1,0:T(8,128)}, s32[1]{0:T(128)}) custom-call(bf16[64,1024]{1,0:T(8,128)(2,1)S(1)} %get-tuple-element.92.cfeat_h, bf16[64,4096]{1,0:T(8,128)(2,1)S(1)} %get-tuple-element.93.sfeat_h, f32[8,128]{1,0:T(8,128)S(1)} %get-tuple-element.94.cmass_h, ...), custom_call_target="tpu_custom_call" | custom-call | tf_op jit(solution)/shard_map/cond/branch_1_fun/pallas_call | solution.py:630
  219.9 41.5 %branch_1_fun.5 = (f32[8,128]{1,0:T(8,128)}, f32[32,128]{1,0:T(8,128)}, f32[64,1024]{1,0:T(8,128)}, f32[64,4096]{1,0:T(8,128)}) custom-call(f32[8,128]{1,0:T(8,128)} %get-tuple-element.97.refs_0_, f32[32,128]{1,0:T(8,128)} %get-tuple-element.98.refs_1_, f32[64,1024]{1,0:T(8,128)} %get-tuple-element.99.refs_2_, f32[64,4096]{1,0:T(8,128)} %get-tuple-element.100.refs_3_), custom_call_target="tpu_custom_call" | custom-call | tf_op jit(solution)/shard_map/cond/branch_1_fun/pallas_call | solution.py:652
Async XLA Ops:
  0.6 0.7 copy-start.3
  0.6 0.7 copy-start.4
  0.7 83.2 %copy-start = (bf16[4096,64]{0,1:T(8,128)(2,1)S(1)}, bf16[4096,64]{0,1:T(8,128)(2,1)}, u32[]{:S(2)}) copy-start(bf16[4096,64]{0,1:T(8,128)(2,1)} %param.8) | copy-start | bytes 1572868
  1.3 82.5 %copy-start.1 = (bf16[1024,64]{0,1:T(8,128)(2,1)S(1)}, bf16[1024,64]{0,1:T(8,128)(2,1)}, u32[]{:S(2)}) copy-start(bf16[1024,64]{0,1:T(8,128)(2,1)} %param.7) | copy-start | bytes 393220
  1.3 82.5 %copy-start.2 = (f32[4096]{0:T(1024)S(1)}, f32[4096]{0:T(1024)}, u32[]{:S(2)}) copy-start(f32[4096]{0:T(1024)} %param.10) | copy-start | bytes 49156

commit v4 on v3

--- a/solution.py
+++ b/solution.py
@@ -95,7 +95,7 @@
     cfeat, sfeat, cmass, smass, pattern, swap_out, swap_in, side_out, side_in, chh, cht, shh, sht, cross, crosst, spread,
     blockmap, slot_peak, peak_scr, list_v, list_s, tab_v, tab_s,
     buf_e, buf_d, flag_e, flag_d, msg_c, rcv_c, msg_s, rcv_s, own_c, own_s, pot_s,
-    sem_swap, sem_e, sem_d, sem_map, sem_loc, sem_in, *more,
+    sem_swap, sem_e, sem_d, sem_map, sem_loc, sem_in, sem_ag, *more,
 ):
     ci = lax.axis_index("cells")
     si = lax.axis_index("spots")
@@ -403,7 +403,7 @@
 
         total = lax.fori_loop(0, cap // step, body, jnp.zeros((SIDE, BLK), F32))
         top = bound[...] + shift
-        return top, jnp.where(total > 0, top + log2(jnp.maximum(total, 1e-38)), NEG)
+        return top, jnp.where(total > 0, top + log2(jnp.maximum(total, 1e-38)), NEG), total
 
     def watch(top, lse):
         near = (top - lse <= GAP) & (lse - top <= 1.5 * GAP) | (top < 0.5 * NEG) & (lse > 0.5 * NEG)
@@ -429,10 +429,10 @@
 
         def iteration(it, carry):
             spots, shift_c, shift_s = carry
-            top, value = quick_half(weight_c, bound_c, spot_log, spots, shift_s, 1, 0)
+            top, value, _ = quick_half(weight_c, bound_c, spot_log, spots, shift_s, 1, 0)
             cell_send(it, value)
             cells = cell_merge(it)
-            top_s, value = quick_half(weight_s, bound_s, cell_log, cells, shift_c, 0, 1)
+            top_s, value, _ = quick_half(weight_s, bound_s, cell_log, cells, shift_c, 0, 1)
             spot_send(it, value)
             lse = settled(cells)
             watch(top, lse)
@@ -443,9 +443,8 @@
             return spots, shift_c, largest(spot_log - lse)
 
         carry = (spots, largest(cells), largest(spot_log - settled(spots)))
-        spots, _, _ = lax.fori_loop(1, ITERS - 1, iteration, carry)
-        lane_spread(spot_log - settled(spots), spread)
-        return jnp.maximum(over_0, jnp.max(worst[...], axis=0, keepdims=True))
+        spots, _, shift_s = lax.fori_loop(1, ITERS - 1, iteration, carry)
+        return over_0, (spots, shift_s)
 
     def first_steps_whole():
         def iteration(it, _):
@@ -458,30 +457,35 @@
             return 0
 
         lax.fori_loop(0, ITERS - 1, iteration, 0)
-        return jnp.zeros((1, BLK), F32)
-
-    over = jnp.maximum(over, first_steps() if quick else first_steps_whole())
-
-    def gather_maps(peak, total, msg, transposed):
-        peak_scr[...] = peak
+        return jnp.zeros((1, BLK), F32), None
+
+    more_over, last = first_steps() if quick else first_steps_whole()
+    over = jnp.maximum(over, more_over)
+
+    def gather_maps(peak, total, msg, transposed, order, send_pair, plain):
+        peak_scr[0] = peak
+        peak_scr[1] = total
         blockmap[cap] = jnp.zeros((FEAT, BLK), F32)
         slot_peak[cap] = jnp.full((1, BLK), NEG, F32)
 
-        def one(b, _):
-            top = peak_scr[pl.ds(b, 1), :]
+        def one(b):
+            top = peak_scr[0, pl.ds(b, 1), :]
             acc = jnp.zeros((FEAT, BLK), F32)
             for k in range(SIDE):
                 e = tab_s[k, core * SIDE + b] if transposed else tab_s[b, core * SIDE + k]
                 e = within(e, cap)
-                acc = acc + blockmap[e] * jnp.exp2(slot_peak[e] - top)
+                acc = acc + (blockmap[e] if plain else blockmap[e] * jnp.exp2(slot_peak[e] - top))
             msg[b, pl.ds(0, FEAT), :] = acc
-            return 0
-
-        lax.fori_loop(0, SIDE, one, 0)
-        for b in range(SIDE):
             msg[b, pl.ds(FEAT, 8), :] = jnp.concatenate(
-                [peak[b : b + 1], total[b : b + 1], jnp.zeros((6, BLK), F32)], axis=0
+                [top, peak_scr[1, pl.ds(b, 1), :], jnp.zeros((6, BLK), F32)], axis=0
             )
+
+        if order is None:
+            lax.fori_loop(0, SIDE, lambda b, _: (one(b), 0)[1], 0)
+        else:
+            for d2 in order:
+                lax.fori_loop(0, 2, lambda h, _: (one(2 * d2 + h), 0)[1], 0)
+                send_pair(d2)
 
     def total_map(take, n):
         top = take(0, pl.ds(FEAT, 8))[0:1]
@@ -496,31 +500,50 @@
             acc = acc + take(k, pl.ds(0, FEAT)) * scale
         return top + log2(total), acc / total
 
-    peak, total = half(crosst, 1, 0, lambda o: shh[mid + o])
-    cell_send(ITERS - 1, joined(peak, total))
-    flag_e[eme] = over
-    for _, dev, _, _ in e_peers:
-        send(flag_e.at[eme], flag_e.at[eme], sem_e.at[0, ITERS], sem_e.at[1, ITERS], dev)
-    gather_maps(peak, total, msg_c, False)
+    def send_flag():
+        flag_e[eme] = jnp.maximum(over, jnp.max(worst[...], axis=0, keepdims=True)) if quick else over
+        for _, dev, _, _ in e_peers:
+            send(flag_e.at[eme], flag_e.at[eme], sem_e.at[0, ITERS], sem_e.at[1, ITERS], dev)
+
+    if quick:
+        last_top, value, total = quick_half(weight_c, bound_c, spot_log, last[0], last[1], 1, 0)
+        cell_send(ITERS - 1, value)
+        peak = last_top
+
+        def quick_maps(i, _):
+            for k in range(step):
+                e = i * step + k
+                o = within(list_s[1, e], SIDE - 1)
+                blockmap[e] = jnp.dot(
+                    shh[mid + o], (weight_c[e] * spread[o]).astype(BF16), preferred_element_type=F32
+                )
+            return 0
+
+        lax.fori_loop(0, cap // step, quick_maps, 0)
+    else:
+        peak, total = half(crosst, 1, 0, lambda o: shh[mid + o])
+        cell_send(ITERS - 1, joined(peak, total))
+        send_flag()
+    gather_maps(peak, total, msg_c, False, None, None, quick)
     for _, dev, s2, k2 in e_peers:
         send(msg_c.at[k2 * 8 + s2], rcv_c.at[eme], sem_map.at[0], sem_map.at[1], dev)
     rcv_c[eme] = msg_c[core * 8 + si]
-    cell_pot = cell_log - settled(cell_merge(ITERS - 1))
+    cell_lse = settled(cell_merge(ITERS - 1))
+    cell_pot = cell_log - cell_lse
     lane_spread(cell_pot, spread)
+    if quick:
+        watch(last_top, cell_lse)
 
     peak, total = half(cross, 0, 1, lambda o: chh[o])
-    gather_maps(peak, total, msg_s, True)
-    for _, dev, d2 in d_peers:
-        send(msg_s.at[pl.ds(d2 * 2, 2)], rcv_s.at[dme], sem_map.at[2], sem_map.at[3], dev)
+    def send_pair(d2):
+        for _, dev, other in d_peers:
+            if other is d2:
+                send(msg_s.at[pl.ds(d2 * 2, 2)], rcv_s.at[dme], sem_map.at[2], sem_map.at[3], dev)
+
+    gather_maps(peak, total, msg_s, True, [d2 for _, _, d2 in d_peers] + [dme], send_pair, False)
     rcv_s[dme] = msg_s[pl.ds(dme * 2, 2)]
-
-    wait_for(flag_e.at[pl.ds(0, 15)], sem_e.at[1, ITERS])
-    over = flag_e[0]
-    for k in range(1, 16):
-        over = jnp.maximum(over, flag_e[k])
-    flag_d[dme] = over
-    for _, dev, _ in d_peers:
-        send(flag_d.at[dme], flag_d.at[dme], sem_d.at[0, ITERS], sem_d.at[1, ITERS], dev)
+    if quick:
+        send_flag()
 
     wait_for(rcv_c.at[pl.ds(0, 15)], sem_map.at[1])
     _, block = total_map(lambda k, r: rcv_c[k, r, :], 16)
@@ -541,11 +564,28 @@
         lses.append(lse)
     pot_s[dme] = jnp.concatenate(lses + [jnp.zeros((6, BLK), F32)], axis=0)
     half_at = core * SIDE * BLK
+
+    def cols_of(d2):
+        return pl.ds(pl.multiple_of(half_at + d2 * 2 * BLK, 2 * BLK), 2 * BLK)
+
+    def pass_on(d2):
+        cols = smap_out.at[:, cols_of(d2)]
+        send(cols, cols, sem_swap.at[6], sem_swap.at[7], partner)
+
     at = pl.ds(pl.multiple_of(half_at + dme * 2 * BLK, 2 * BLK), 2 * BLK)
     smap_out[:, at] = own_s[...]
     for _, dev, _ in d_peers:
         send(pot_s.at[dme], pot_s.at[dme], sem_map.at[6], sem_map.at[7], dev)
-        send(own_s, smap_out.at[:, at], sem_map.at[8], sem_map.at[9], dev)
+        send(own_s, smap_out.at[:, at], sem_map.at[8], sem_ag.at[dme], dev)
+
+    pass_on(dme)
+    wait_for(flag_e.at[pl.ds(0, 15)], sem_e.at[1, ITERS])
+    over = flag_e[0]
+    for k in range(1, 16):
+        over = jnp.maximum(over, flag_e[k])
+    flag_d[dme] = over
+    for _, dev, _ in d_peers:
+        send(flag_d.at[dme], flag_d.at[dme], sem_d.at[0, ITERS], sem_d.at[1, ITERS], dev)
 
     cell_norm = jnp.zeros((8, BLK), F32)
     rows8 = lax.broadcasted_iota(jnp.int32, (8, BLK), 0)
@@ -562,10 +602,9 @@
     half_rows = pl.ds(pl.multiple_of(core * SIDE, SIDE), SIDE)
     spot_out[half_rows, :] = (spot_log - lse + spot_norm) * (1.0 / UNIT)
     send(spot_out.at[half_rows], spot_out.at[half_rows], sem_swap.at[4], sem_swap.at[5], partner)
-    half_cols = pl.ds(pl.multiple_of(half_at, SIDE * BLK), SIDE * BLK)
-    part = smap_out.at[:, pl.ds(0, 7 * 2 * BLK)]
-    wait_for(part, sem_map.at[9])
-    send(smap_out.at[:, half_cols], smap_out.at[:, half_cols], sem_swap.at[6], sem_swap.at[7], partner)
+    for _, _, d2 in reversed(d_peers):
+        wait_for(own_s, sem_ag.at[d2])
+        pass_on(d2)
 
     wait_for(flag_d.at[pl.ds(0, 7)], sem_d.at[1, ITERS])
     over = flag_d[0]
@@ -584,7 +623,7 @@
     wait_for(rcv_s.at[pl.ds(0, 7)], sem_map.at[2])
     wait_for(cmap_out.at[:, pl.ds(0, 7 * BLK)], sem_map.at[4])
     wait_for(pot_s.at[pl.ds(0, 7)], sem_map.at[6])
-    wait_for(part, sem_map.at[8])
+    wait_for(smap_out.at[:, pl.ds(0, 7 * 2 * BLK)], sem_map.at[8])
     wait_for(flag_e.at[pl.ds(0, 15)], sem_e.at[0, ITERS])
     wait_for(flag_d.at[pl.ds(0, 7)], sem_d.at[0, ITERS])
 
@@ -611,7 +650,7 @@
         vmem(8, FEAT, BLK), vmem(8, FEAT, BLK), vmem(2, 8, BLK), vmem(2, 8, BLK),
         half(SIDE, FEAT, BLK), half(SIDE, BLK, FEAT), half(spots, FEAT, BLK), half(spots, BLK, DEEP if quick else FEAT),
         vmem(cap, BLK, BLK), vmem(cap, BLK, BLK), vmem(SIDE, BLK, BLK),
-        vmem(cap + 1, FEAT, BLK), vmem(cap + 1, 1, BLK), vmem(SIDE, BLK),
+        vmem(cap + 1, FEAT, BLK), vmem(cap + 1, 1, BLK), vmem(2, SIDE, BLK),
         pltpu.VMEM((8, width), jnp.int32), pltpu.SMEM((8, width), jnp.int32),
         pltpu.VMEM((SIDE, BLK), jnp.int32), pltpu.SMEM((SIDE, BLK), jnp.int32),
         vmem(ITERS, 16, SIDE, BLK), vmem(ITERS - 1, 8, SIDE, BLK), vmem(16, 8, BLK), vmem(8, 8, BLK),
@@ -619,7 +658,7 @@
         vmem(FEAT, BLK), vmem(FEAT, 2 * BLK), vmem(8, 8, BLK),
         pltpu.SemaphoreType.DMA((8,)), pltpu.SemaphoreType.DMA((2, ITERS + 1)),
         pltpu.SemaphoreType.DMA((2, ITERS + 1)), pltpu.SemaphoreType.DMA((10,)),
-        pltpu.SemaphoreType.DMA((3,)), pltpu.SemaphoreType.DMA((5,)),
+        pltpu.SemaphoreType.DMA((3,)), pltpu.SemaphoreType.DMA((5,)), pltpu.SemaphoreType.DMA((8,)),
     ]
     if quick:
         scratch += [

time: 262 us -> 260 us (level)
  no operation moved by 1% of the time
where the time goes in v4:
time: 260 us
  Pallas kernels  258 us (99%)
    pallas_call x2, Pallas kernels, run(): pl.pallas_call(functools.partial(sinkhorn_kernel, cap, quick), out_shape=...  216 us
    pallas_call x1, Pallas kernels, place(): pl.pallas_call(place_kernel, out_shape=tuple((jax.ShapeDtypeStruct(a.shap...  41.5 us

profile of v4, /device:TPU:1, one launch (start us, length us, event | category | flops | bytes accessed | tf_op | source)
XLA Modules:
  0.0 259.9 jit_solution(9455322358351157917)
XLA Ops:
  0.6 0.0 copy-start.3
  0.6 0.0 copy-start.4
  0.7 0.0 copy-start
  0.7 0.7 copy-done.3
  1.3 0.0 copy-done.4
  1.3 0.0 copy-start.1
  1.3 0.0 copy-start.2
  1.3 81.0 %shard_map.84 = (f32[8,128]{1,0:T(8,128)S(1)}, f32[32,128]{1,0:T(8,128)S(1)}, f32[64,1024]{1,0:T(8,128)S(1)}, f32[64,4096]{1,0:T(8,128)S(1)}, s32[1]{0:T(128)}) custom-call(bf16[64,1024]{1,0:T(8,128)(2,1)} %bitcast.11, bf16[64,4096]{1,0:T(8,128)(2,1)} %bitcast.9, f32[8,128]{1,0:T(8,128)S(1)} %bitcast.15, f32[32,128]{1,0:T(8,128)} %bitcast.13, ...), custom_call_target="tpu_custom_call" | custom-call | tf_op jit(solution)/shard_map/pallas_call | solution.py:669
  82.9 0.0 copy-done
  82.9 0.0 copy-done.1
  83.0 0.0 copy-done.2
  83.0 177.0 %conditional.1 = ((f32[8,128]{1,0:T(8,128)}, f32[32,128]{1,0:T(8,128)}, f32[64,1024]{1,0:T(8,128)}, f32[64,4096]{1,0:T(8,128)})) conditional(s32[]{:T(128)} %bitcast.4, (f32[8,128]{1,0:T(8,128)S(1)}, f32[32,128]{1,0:T(8,128)S(1)}, f32[64,1024]{1,0:T(8,128)S(1)}, f32[64,4096]{1,0:T(8,128)S(1)}) %tuple.25, (bf16[64,1024]{1,0:T(8,128)(2,1)S(1)}, ...), branch_computations={%region_0.0_spmd.clone, %region_1.0_spmd.clone} | conditional | bytes 8 | solution.py:703
  83.0 135.5 %branch_1_fun.4 = (f32[8,128]{1,0:T(8,128)}, f32[32,128]{1,0:T(8,128)}, f32[64,1024]{1,0:T(8,128)}, f32[64,4096]{1,0:T(8,128)}, s32[1]{0:T(128)}) custom-call(bf16[64,1024]{1,0:T(8,128)(2,1)S(1)} %get-tuple-element.92.cfeat_h, bf16[64,4096]{1,0:T(8,128)(2,1)S(1)} %get-tuple-element.93.sfeat_h, f32[8,128]{1,0:T(8,128)S(1)} %get-tuple-element.94.cmass_h, ...), custom_call_target="tpu_custom_call" | custom-call | tf_op jit(solution)/shard_map/cond/branch_1_fun/pallas_call | solution.py:669
  218.5 41.5 %branch_1_fun.5 = (f32[8,128]{1,0:T(8,128)}, f32[32,128]{1,0:T(8,128)}, f32[64,1024]{1,0:T(8,128)}, f32[64,4096]{1,0:T(8,128)}) custom-call(f32[8,128]{1,0:T(8,128)} %get-tuple-element.97.refs_0_, f32[32,128]{1,0:T(8,128)} %get-tuple-element.98.refs_1_, f32[64,1024]{1,0:T(8,128)} %get-tuple-element.99.refs_2_, f32[64,4096]{1,0:T(8,128)} %get-tuple-element.100.refs_3_), custom_call_target="tpu_custom_call" | custom-call | tf_op jit(solution)/shard_map/cond/branch_1_fun/pallas_call | solution.py:691
Async XLA Ops:
  0.6 0.7 copy-start.3
  0.6 0.7 copy-start.4
  0.7 82.3 %copy-start = (bf16[4096,64]{0,1:T(8,128)(2,1)S(1)}, bf16[4096,64]{0,1:T(8,128)(2,1)}, u32[]{:S(2)}) copy-start(bf16[4096,64]{0,1:T(8,128)(2,1)} %param.8) | copy-start | bytes 1572868
  1.3 81.6 %copy-start.1 = (bf16[1024,64]{0,1:T(8,128)(2,1)S(1)}, bf16[1024,64]{0,1:T(8,128)(2,1)}, u32[]{:S(2)}) copy-start(bf16[1024,64]{0,1:T(8,128)(2,1)} %param.7) | copy-start | bytes 393220
  1.3 81.6 %copy-start.2 = (f32[4096]{0:T(1024)S(1)}, f32[4096]{0:T(1024)}, u32[]{:S(2)}) copy-start(f32[4096]{0:T(1024)} %param.10) | copy-start | bytes 49156

commit v5 on v4

--- a/solution.py
+++ b/solution.py
@@ -506,20 +506,23 @@
             send(flag_e.at[eme], flag_e.at[eme], sem_e.at[0, ITERS], sem_e.at[1, ITERS], dev)
 
     if quick:
-        last_top, value, total = quick_half(weight_c, bound_c, spot_log, last[0], last[1], 1, 0)
+        last_top, value, _ = quick_half(weight_c, bound_c, spot_log, last[0], last[1], 1, 0)
         cell_send(ITERS - 1, value)
         peak = last_top
 
-        def quick_maps(i, _):
+        def quick_maps(i, total):
+            parts = []
             for k in range(step):
                 e = i * step + k
                 o = within(list_s[1, e], SIDE - 1)
-                blockmap[e] = jnp.dot(
-                    shh[mid + o], (weight_c[e] * spread[o]).astype(BF16), preferred_element_type=F32
-                )
-            return 0
-
-        lax.fori_loop(0, cap // step, quick_maps, 0)
+                p = (weight_c[e] * spread[o]).astype(BF16)
+                blockmap[e] = jnp.dot(shh[mid + o], p, preferred_element_type=F32)
+                parts.append((list_s[2, e], jnp.sum(p.astype(F32), axis=0, keepdims=True)))
+            for at, part in parts:
+                total = total + jnp.where(rows == at, part, 0.0)
+            return total
+
+        total = lax.fori_loop(0, cap // step, quick_maps, jnp.zeros((SIDE, BLK), F32))
     else:
         peak, total = half(crosst, 1, 0, lambda o: shh[mid + o])
         cell_send(ITERS - 1, joined(peak, total))

time: 260 us -> 260 us (level)
  no operation moved by 1% of the time
where the time goes in v5:
time: 260 us
  Pallas kernels  258 us (99%)
    pallas_call x2, Pallas kernels, run(): pl.pallas_call(functools.partial(sinkhorn_kernel, cap, quick), out_shape=...  217 us
    pallas_call x1, Pallas kernels, place(): pl.pallas_call(place_kernel, out_shape=tuple((jax.ShapeDtypeStruct(a.shap...  41.5 us

profile of v5, /device:TPU:1, one launch (start us, length us, event | category | flops | bytes accessed | tf_op | source)
XLA Modules:
  0.0 260.0 jit_solution(4338929428561955349)
XLA Ops:
  0.6 0.0 copy-start.3
  0.6 0.0 copy-start.4
  0.7 0.0 copy-start
  0.7 0.7 copy-done.3
  1.3 0.0 copy-done.4
  1.3 0.0 copy-start.1
  1.3 0.0 copy-start.2
  1.3 80.9 %shard_map.84 = (f32[8,128]{1,0:T(8,128)S(1)}, f32[32,128]{1,0:T(8,128)S(1)}, f32[64,1024]{1,0:T(8,128)S(1)}, f32[64,4096]{1,0:T(8,128)S(1)}, s32[1]{0:T(128)}) custom-call(bf16[64,1024]{1,0:T(8,128)(2,1)} %bitcast.11, bf16[64,4096]{1,0:T(8,128)(2,1)} %bitcast.9, f32[8,128]{1,0:T(8,128)S(1)} %bitcast.15, f32[32,128]{1,0:T(8,128)} %bitcast.13, ...), custom_call_target="tpu_custom_call" | custom-call | tf_op jit(solution)/shard_map/pallas_call | solution.py:672
  82.9 0.0 copy-done
  82.9 0.0 copy-done.1
  83.0 0.0 copy-done.2
  83.0 177.1 %conditional.1 = ((f32[8,128]{1,0:T(8,128)}, f32[32,128]{1,0:T(8,128)}, f32[64,1024]{1,0:T(8,128)}, f32[64,4096]{1,0:T(8,128)})) conditional(s32[]{:T(128)} %bitcast.4, (f32[8,128]{1,0:T(8,128)S(1)}, f32[32,128]{1,0:T(8,128)S(1)}, f32[64,1024]{1,0:T(8,128)S(1)}, f32[64,4096]{1,0:T(8,128)S(1)}) %tuple.25, (bf16[64,1024]{1,0:T(8,128)(2,1)S(1)}, ...), branch_computations={%region_0.0_spmd.clone, %region_1.0_spmd.clone} | conditional | bytes 8 | solution.py:706
  83.0 135.6 %branch_1_fun.4 = (f32[8,128]{1,0:T(8,128)}, f32[32,128]{1,0:T(8,128)}, f32[64,1024]{1,0:T(8,128)}, f32[64,4096]{1,0:T(8,128)}, s32[1]{0:T(128)}) custom-call(bf16[64,1024]{1,0:T(8,128)(2,1)S(1)} %get-tuple-element.92.cfeat_h, bf16[64,4096]{1,0:T(8,128)(2,1)S(1)} %get-tuple-element.93.sfeat_h, f32[8,128]{1,0:T(8,128)S(1)} %get-tuple-element.94.cmass_h, ...), custom_call_target="tpu_custom_call" | custom-call | tf_op jit(solution)/shard_map/cond/branch_1_fun/pallas_call | solution.py:672
  218.6 41.5 %branch_1_fun.5 = (f32[8,128]{1,0:T(8,128)}, f32[32,128]{1,0:T(8,128)}, f32[64,1024]{1,0:T(8,128)}, f32[64,4096]{1,0:T(8,128)}) custom-call(f32[8,128]{1,0:T(8,128)} %get-tuple-element.97.refs_0_, f32[32,128]{1,0:T(8,128)} %get-tuple-element.98.refs_1_, f32[64,1024]{1,0:T(8,128)} %get-tuple-element.99.refs_2_, f32[64,4096]{1,0:T(8,128)} %get-tuple-element.100.refs_3_), custom_call_target="tpu_custom_call" | custom-call | tf_op jit(solution)/shard_map/cond/branch_1_fun/pallas_call | solution.py:694
Async XLA Ops:
  0.6 0.7 copy-start.3
  0.6 0.7 copy-start.4
  0.7 82.3 %copy-start = (bf16[4096,64]{0,1:T(8,128)(2,1)S(1)}, bf16[4096,64]{0,1:T(8,128)(2,1)}, u32[]{:S(2)}) copy-start(bf16[4096,64]{0,1:T(8,128)(2,1)} %param.8) | copy-start | bytes 1572868
  1.3 81.6 %copy-start.1 = (bf16[1024,64]{0,1:T(8,128)(2,1)S(1)}, bf16[1024,64]{0,1:T(8,128)(2,1)}, u32[]{:S(2)}) copy-start(bf16[1024,64]{0,1:T(8,128)(2,1)} %param.7) | copy-start | bytes 393220
  1.3 81.6 %copy-start.2 = (f32[4096]{0:T(1024)S(1)}, f32[4096]{0:T(1024)}, u32[]{:S(2)}) copy-start(f32[4096]{0:T(1024)} %param.10) | copy-start | bytes 49156
